TPU v7x, 32 devices: a whole 2x2x4 slice. The times are simulated.
32 devices in a mesh: tok: 4 (over z), blk: 8 (over y, x, core).
Axes of the slice: x: 2, y: 2, z: 4, core: 2. Of those that a mesh axis runs over, the one named last changes fastest.
Arguments:
- acts: bfloat16 [512, 8192], P('tok', 'blk'), may hold values from -35 to 35
- out_grad: bfloat16 [512, 29568], P(('tok', 'blk')), may hold values from -0.12 to 0.12
- kept_ids: int32 [8, 16], replicated, may hold values from 0 to 14783, as said below
- cand_ids: int32 [8, 48], replicated, may hold values from 0 to 14783, as said below
Outputs:
- kept_grad: bfloat16 [8, 16, 128, 128], P('blk', 'tok')
- cand_score: float32 [8, 48], P('blk', 'tok')
Inputs may be any that keep to these rules, and one draw needn't show every extreme that they name: `kept_ids`: within one owner's kept and candidate blocks every block id appears once; one owner's blocks use at most 58 distinct block columns, exactly 58 for some owner, and no block column is used by two owners. `cand_ids`: numbered and owned as the kept blocks, and distinct from them.
All inputs are finite; a program needn't handle non-finite values.
Results may differ from a plain program's by a relative error of at most 0.001.
Values may be sent and summed in bfloat16 or wider, within the bound.
No kernel may reach another device: no remote copies, remote signals or barrier semaphores. Data moves between devices by JAX's collectives and lax.ppermute only.
A program may use at most 64 MiB of HBM per device.

v0:
```python
import jax
import jax.numpy as jnp
from jax import lax
from jax.sharding import PartitionSpec as P

BLOCK = 128
KS = 16


def column_table(slot_cols, width):
    return jax.vmap(lambda cols: jnp.unique(cols, size=width, fill_value=0))(slot_cols).astype(
        jnp.int32
    )


def local(acts, out_grad, kept_ids, cand_ids):
    owners = lax.axis_size("blk")
    tok_count = lax.axis_size("tok")
    owner_index = lax.axis_index("blk")
    ncols = out_grad.shape[1] // BLOCK
    width = 2 * ((ncols + owners - 1) // owners)
    slot_ids = jnp.concatenate([kept_ids, cand_ids], axis=1)
    table = column_table(slot_ids % ncols, width)
    local_rows = out_grad.shape[0]
    grad3 = out_grad.reshape(local_rows, ncols, BLOCK)
    outgoing = jnp.take(grad3, table.reshape(-1), axis=1).reshape(local_rows, owners, width, BLOCK)
    incoming = lax.all_to_all(outgoing, "blk", split_axis=1, concat_axis=0, tiled=True)
    grad_cols = incoming.reshape(-1, width, BLOCK)
    acts_all = lax.all_gather(acts, "blk", axis=1, tiled=True)
    nrows = acts_all.shape[1] // BLOCK
    acts3 = acts_all.reshape(acts_all.shape[0], nrows, BLOCK)
    my_ids = lax.dynamic_index_in_dim(slot_ids, owner_index, 0, keepdims=False)
    my_table = lax.dynamic_index_in_dim(table, owner_index, 0, keepdims=False)
    row_index = my_ids // ncols
    matches = my_table[None, :] == (my_ids % ncols)[:, None]
    col_index = jnp.argmax(matches, axis=1)

    def one_group(indices):
        rows_here, cols_here = indices
        left = jnp.take(acts3, rows_here, axis=1)
        right = jnp.take(grad_cols, cols_here, axis=1)
        return jnp.einsum("tgi,tgj->gij", left, right, preferred_element_type=jnp.float32)

    total_slots = my_ids.shape[0]
    partials = lax.map(one_group, (row_index.reshape(-1, 16), col_index.reshape(-1, 16)))
    partials = partials.reshape(total_slots, BLOCK, BLOCK)
    kept_part = partials[:KS]
    cand_part = partials[KS:]
    kept_full, cand_full = lax.psum((kept_part, cand_part), "tok")
    tok_index = lax.axis_index("tok")
    kept_share = KS // tok_count
    cand_share = cand_part.shape[0] // tok_count
    kept_sum = lax.dynamic_slice_in_dim(kept_full, tok_index * kept_share, kept_share, 0)
    cand_sum = lax.dynamic_slice_in_dim(cand_full, tok_index * cand_share, cand_share, 0)
    kept_grad = kept_sum.astype(jnp.bfloat16)[None]
    norms = jnp.sqrt(jnp.sum(cand_sum * cand_sum, axis=(1, 2)))
    peak = lax.pmax(jnp.max(norms), ("tok", "blk"))
    cand_score = (norms / (peak + 1e-06))[None]
    return (kept_grad, cand_score)


def solution(mesh):
    return jax.shard_map(
        local,
        mesh=mesh,
        in_specs=(P("tok", "blk"), P(("tok", "blk"), None), P(), P()),
        out_specs=(P("blk", "tok", None, None), P("blk", "tok")),
        check_vma=False,
    )
```

profile of v0, /device:TPU:0, one launch (start us, length us, event | category | flops | bytes accessed | tf_op | source)
XLA Modules:
  0.0 319.6 jit_solution(1479462801111851287)
XLA Ops:
  7.2 1.9 copy.80
  11.5 2.6 gather_fusion.3
  14.8 6.7 %fusion.12 = s32[8,64,1]{2,0,1:T(8,128)S(1)} fusion(s32[8,64,1]{2,0,1:T(8,128)S(1)} %copy.87), kind=kOutput, calls=%fused_computation.40 | output fusion | flops 38400 | bytes 4096 | tf_op jit(solution)/shard_map/vmap(jit(cumsum))/reduce_window_sum | solution.py:11
  21.7 22.3 %scatter_fusion = s32[8,58]{1,0:T(8,128)S(1)} fusion(s32[8,58]{1,0:T(8,128)S(1)} %broadcast_in_dim.81, s32[512]{0:T(512)S(1)} %reshape.355, s32[512]{0:T(512)S(1)} %broadcast.332), kind=kCustom, calls=%fused_computation.5 | custom fusion | flops 512 | bytes 10240 | tf_op jit(solution)/shard_map/vmap()/scatter-add | solution.py:11
  44.6 3.9 %gather_fusion.4 = s32[464]{0:T(512)S(1)} fusion(s32[8,64]{1,0:T(8,128)S(1)} %reshape.346, s32[464]{0:T(512)S(1)} %reshape.349), kind=kCustom, calls=%fused_computation.4 | custom fusion | bytes 7424 | tf_op jit(solution)/shard_map/vmap()/gather | solution.py:11
  48.9 2.7 gather_fusion.2
  51.6 2.8 broadcast_select_fusion
  54.4 5.2 %all-to-all-start = ((bf16[16,8,58,128]{3,0,2,1:T(8,128)(2,1)}), bf16[16,8,58,128]{3,0,2,1:T(8,128)(2,1)S(1)}, u32[]{:S(2)}, u32[]{:S(2)}) async-start(bf16[16,8,58,128]{3,0,2,1:T(8,128)(2,1)} %broadcast_select_fusion), calls=%async_computation | async-start | bytes 3801088 | tf_op jit(solution)/shard_map/all_to_all | solution.py:27
  60.7 23.4 %all-to-all-done = bf16[16,8,58,128]{3,0,2,1:T(8,128)(2,1)S(1)} async-done(((bf16[16,8,58,128]{3,0,2,1:T(8,128)(2,1)}), bf16[16,8,58,128]{3,0,2,1:T(8,128)(2,1)S(1)}, u32[]{:S(2)}, u32[]{:S(2)}) %all-to-all-start) | async-done | bytes 1900576 | tf_op jit(solution)/shard_map/all_to_all | solution.py:27
  84.1 1.9 copy.92
  86.0 4.1 %copy.93 = bf16[128,64,128]{2,0,1:T(8,128)(2,1)} copy(bf16[128,64,128]{0,2,1:T(8,128)(2,1)} %bitcast.76) | data formatting | bytes 4194304 | tf_op jit(solution)/shard_map/while | solution.py:45
  90.0 23.6 %while.11 = (s32[]{:T(128)}, f32[4,16,128,128]{3,2,1,0:T(8,128)}, s32[4,16]{1,0:T(4,128)S(1)}, bf16[128,64,128]{2,0,1:T(8,128)(2,1)}, s32[4,16]{1,0:T(4,128)S(1)}, /*index=5*/bf16[128,58,128]{2,0,1:T(8,128)(2,1)}, s32[]{:T(128)}) while((s32[]{:T(128)}, f32[4,16,128,128]{3,2,1,0:T(8,128)}, s32[4,16]{1,0:T(4,128)S(1)}, ...), condition=%wide.region_7.8_spmd, body=%wide.region_6.7_spmd.sunk | while | flops 67635488 | bytes 4203797 | solution.py:45
  90.1 2.2 gather_fusion
  92.2 2.2 gather_fusion.1
  96.0 2.2 gather_fusion
  98.1 2.2 gather_fusion.1
  101.9 2.2 gather_fusion
  104.1 2.2 gather_fusion.1
  107.8 2.2 gather_fusion
  110.0 2.2 gather_fusion.1
  113.6 4.0 %slice.40 = f32[3,16,128,128]{3,2,1,0:T(8,128)} slice(f32[4,16,128,128]{3,2,1,0:T(8,128)} %get-tuple-element.50), slice={[1:4], [0:16], [0:128], [0:128]} | slice | bytes 6291456 | tf_op jit(solution)/shard_map/slice | solution.py:48
  118.9 75.6 %all-reduce.5 = bf16[16,128,128]{2,1,0:T(8,128)(2,1)S(1)} all-reduce(f32[16,128,128]{2,1,0:T(8,128)S(1)} %slice_bitcast_fusion), channel_id=1, replica_groups=mesh['tok'=4,'blk'=8] {'tok'}, use_global_device_ids=true, to_apply=%region_8.9 | all-reduce | flops 262144 | bytes 1572864 | tf_op jit(solution)/shard_map/psum | solution.py:49
  194.5 75.1 %all-reduce.4.cloned.1.call-done = f32[48,128,128]{2,1,0:T(8,128)} async-done(((f32[48,128,128]{2,1,0:T(8,128)}), f32[48,128,128]{2,1,0:T(8,128)}) %all-reduce.4.cloned.1.call-update) | async-done | bytes 3145744 | tf_op jit(solution)/shard_map/psum | solution.py:49
  272.2 39.4 %pmax.7 = f32[]{:T(128)} all-reduce(f32[]{:T(128)} %sqrt_reduce_fusion), channel_id=1, replica_groups=mesh['tok'=4,'blk'=8] {'tok','blk'}, use_global_device_ids=true, to_apply=%region_12.13 | all-reduce | flops 1 | bytes 8 | tf_op jit(solution)/shard_map/pmax | solution.py:57
  (71 shorter events, 15.7 us)
Async XLA Ops:
  7.2 41.5 %copy-start = (bf16[16,29568]{1,0:T(8,128)(2,1)S(1)}, bf16[16,29568]{1,0:T(8,128)(2,1)}, u32[]{:S(2)}) copy-start(bf16[16,29568]{1,0:T(8,128)(2,1)} %param.9) | copy-start | bytes 2838532
  7.2 78.8 %all-gather.2.cloned.1.call-start = ((), (), s32[]{:S(2)}) async-start(), calls=%async_computation.1 | async-start | bytes 2359296 | tf_op jit(solution)/shard_map/all_gather | solution.py:29
  54.4 29.7 %all-to-all-start = ((bf16[16,8,58,128]{3,0,2,1:T(8,128)(2,1)}), bf16[16,8,58,128]{3,0,2,1:T(8,128)(2,1)S(1)}, u32[]{:S(2)}, u32[]{:S(2)}) async-start(bf16[16,8,58,128]{3,0,2,1:T(8,128)(2,1)} %broadcast_select_fusion), calls=%async_computation | async-start | bytes 3801088 | tf_op jit(solution)/shard_map/all_to_all | solution.py:27
  59.6 210.0 %all-reduce.4.cloned.1.call-start = ((), (), s32[]{:S(2)}) async-start(), calls=%async_computation.2 | async-start | bytes 6291456 | tf_op jit(solution)/shard_map/psum | solution.py:49
Sparse Core Ops, SparseCore 0:
  9.9 30.6 all-gather.1
  117.8 151.7 all-reduce.3
where the time goes:
time: 320 us
  blocking collectives  115 us (36%)
  waiting for transfers between devices  98.5 us (31%)
  local copies, waits for them, and re-layouts  42.6 us (13%)
  other arithmetic  37.6 us (12%)
  between operations  14.9 us (5%)
  matrix products  5.71 us (2%)
  starting transfers between devices  5.25 us (2%)
    psum x1, blocking collectives, local(): kept_full, cand_full = lax.psum((kept_part, cand_part), 'tok')  75.6 us
    psum x1, waiting for transfers between devices, local(): kept_full, cand_full = lax.psum((kept_part, cand_part), 'tok')  75.1 us
    pmax x1, blocking collectives, local(): peak = lax.pmax(jnp.max(norms), ('tok', 'blk'))  39.4 us
    all_to_all x1, waiting for transfers between devices, local(): lax.all_to_all(outgoing, 'blk', split_axis=1, concat_axis=0, tiled=True)  23.4 us
    scatter-add x1, other arithmetic, column_table(): jnp.unique(cols, size=width, fill_value=0)  22.3 us
    gather x4, local copies, waits for them, and re-layouts, one_group(): left = jnp.take(acts3, rows_here, axis=1)  8.96 us
    gather x4, local copies, waits for them, and re-layouts, one_group(): right = jnp.take(grad_cols, cols_here, axis=1)  8.68 us
    gather x9, local copies, waits for them, and re-layouts, column_table(): jnp.unique(cols, size=width, fill_value=0)  7.3 us
  transfers between devices with their start and end apart: 3, of which 2 were waited for; matrix products, arithmetic and copies ran while one was open for 15% of the time, Pallas kernels for 0%

commit v1 on v0

v1 whole, which is shorter than its diff:
```python
import functools

import jax
import jax.numpy as jnp
from jax import lax
from jax.experimental import pallas as pl
from jax.experimental.pallas import tpu as pltpu
from jax.sharding import PartitionSpec as P

BLOCK = 128
TILE_ROWS = 16
VMEM_LIMIT = 40 * 1024 * 1024
ANY = pl.BlockSpec(memory_space=pl.ANY)
VMEM = pl.BlockSpec(memory_space=pltpu.VMEM)
SMEM = pl.BlockSpec(memory_space=pltpu.SMEM)


def swap(x, axis, mask):
    size = lax.axis_size(axis)
    return lax.ppermute(x, axis, [(i, i ^ mask) for i in range(size)])


def transpose_kernel(src, dst):
    for row in range(src.shape[1] // BLOCK):
        here = pl.ds(row * BLOCK, BLOCK)
        dst[here, :] = src[:, here].T


def transpose_acts(acts):
    tokens, width = acts.shape
    return pl.pallas_call(
        transpose_kernel,
        out_shape=jax.ShapeDtypeStruct((width, tokens), acts.dtype),
        in_specs=[VMEM],
        out_specs=VMEM,
        compiler_params=pltpu.CompilerParams(vmem_limit_bytes=VMEM_LIMIT),
    )(acts)


def gather_kernel(owners, chunks, pos, cols, grad, *outs):
    rows = grad.shape[0]
    me = pos[0]
    for which, slots in enumerate(chunks):
        for peer in range(owners):
            out = outs[which * owners + peer]
            dest = me ^ peer
            for k, slot in enumerate(slots):
                start = pl.multiple_of(cols[dest, slot] * BLOCK, BLOCK)
                out[k] = grad[:, pl.ds(start, BLOCK)]


def gather_columns(out_grad, cols, pos, owners, chunks):
    rows = out_grad.shape[0]
    if rows % TILE_ROWS:
        grad3 = out_grad.reshape(rows, -1, BLOCK)
        return [
            jnp.swapaxes(jnp.take(grad3, cols[pos[0] ^ peer][jnp.array(slots)], axis=1), 0, 1)
            for slots in chunks
            for peer in range(owners)
        ]
    return pl.pallas_call(
        functools.partial(gather_kernel, owners, chunks),
        out_shape=[
            jax.ShapeDtypeStruct((len(slots), rows, BLOCK), out_grad.dtype)
            for slots in chunks
            for _ in range(owners)
        ],
        in_specs=[SMEM, SMEM, VMEM],
        out_specs=[VMEM] * (owners * len(chunks)),
        compiler_params=pltpu.CompilerParams(vmem_limit_bytes=VMEM_LIMIT),
    )(pos, cols, out_grad)


def product_kernel(owners, pieces, toks, share, first, pos, rows, *refs):
    acts = refs[:owners]
    grads = refs[owners : owners + pieces]
    outs = refs[owners + pieces : owners + pieces + toks]
    acts_all, grad_all, sem = refs[owners + pieces + toks :]
    me, tok = pos[0], pos[1]
    width = acts[0].shape[0]
    part = grads[0].shape[1]
    copies = []
    for peer in range(owners):
        src = me ^ peer
        copies.append(
            pltpu.make_async_copy(
                acts[peer],
                acts_all.at[pl.ds(pl.multiple_of(src * width, width), width)],
                sem.at[0, peer],
            )
        )
    for peer in range(pieces):
        src = me ^ peer if pieces > 1 else 0
        copies.append(
            pltpu.make_async_copy(
                grads[peer],
                grad_all.at[:, pl.ds(pl.multiple_of(src * part, part), part)],
                sem.at[1, peer],
            )
        )
    for copy in copies:
        copy.start()
    for copy in copies:
        copy.wait()
    for peer in range(toks):
        unit = tok ^ peer
        for k in range(share):
            slot = unit * share + k
            row = rows[first(unit) + k]
            left = acts_all[pl.ds(pl.multiple_of(row * BLOCK, BLOCK), BLOCK), :]
            prod = jnp.dot(left, grad_all[slot], preferred_element_type=jnp.float32)
            outs[peer][k] = prod.astype(outs[peer].dtype)


def products(acts, grads, rows, pos, toks, share, first, dtype):
    owners = len(acts)
    slots, part, _ = grads[0].shape
    tokens = acts[0].shape[1]
    if part % TILE_ROWS:
        order = pos[0] ^ jnp.arange(owners)
        whole = jnp.swapaxes(jnp.take(jnp.stack(grads), order, axis=0), 0, 1)
        grads = [whole.reshape(slots, tokens, BLOCK)]
    return pl.pallas_call(
        functools.partial(product_kernel, owners, len(grads), toks, share, first),
        out_shape=[
            jax.ShapeDtypeStruct((share, BLOCK, BLOCK), jnp.float32 if peer == 0 else dtype)
            for peer in range(toks)
        ],
        in_specs=[SMEM, SMEM] + [ANY] * (owners + len(grads)),
        out_specs=[VMEM] * toks,
        scratch_shapes=[
            pltpu.VMEM((owners * acts[0].shape[0], tokens), acts[0].dtype),
            pltpu.VMEM((slots, tokens, BLOCK), grads[0].dtype),
            pltpu.SemaphoreType.DMA((2, owners)),
        ],
        compiler_params=pltpu.CompilerParams(vmem_limit_bytes=VMEM_LIMIT),
    )(pos, rows, *acts, *grads)


def norm_kernel(counts, toks, *refs):
    norms, peak = refs[-2:]
    norms[...] = jnp.zeros_like(norms)
    at = 0
    for which, count in enumerate(counts):
        parts = refs[which * toks : (which + 1) * toks]
        for k in range(count):
            total = parts[0][k]
            for other in parts[1:]:
                total = total + other[k].astype(jnp.float32)
            norms[at : at + 1, :] = jnp.sum(total * total, axis=0, keepdims=True)
            at += 1
    each = jnp.sqrt(jnp.sum(norms[...], axis=1, keepdims=True))
    norms[...] = jnp.broadcast_to(each, norms.shape)
    peak[...] = jnp.broadcast_to(jnp.max(each, axis=0, keepdims=True), peak.shape)


def block_norms(parts, counts):
    toks = len(parts[0])
    height = -(-sum(counts) // 8) * 8
    return pl.pallas_call(
        functools.partial(norm_kernel, counts, toks),
        out_shape=[
            jax.ShapeDtypeStruct((height, BLOCK), jnp.float32),
            jax.ShapeDtypeStruct((8, BLOCK), jnp.float32),
        ],
        in_specs=[VMEM] * (toks * len(counts)),
        out_specs=[VMEM] * 2,
        compiler_params=pltpu.CompilerParams(vmem_limit_bytes=VMEM_LIMIT),
    )(*[x for chunk in parts for x in chunk])


def kept_kernel(*refs):
    total = refs[0][...]
    for other in refs[1:-1]:
        total = total + other[...]
    refs[-1][0] = total.astype(refs[-1].dtype)


def kept_sum(parts):
    return pl.pallas_call(
        kept_kernel,
        out_shape=jax.ShapeDtypeStruct((1,) + parts[0].shape, jnp.bfloat16),
        in_specs=[VMEM] * len(parts),
        out_specs=VMEM,
        compiler_params=pltpu.CompilerParams(vmem_limit_bytes=VMEM_LIMIT),
    )(*parts)


def global_peak(peak):
    mask = 1
    while mask < lax.axis_size("blk"):
        peak = jnp.maximum(peak, swap(peak, "blk", mask))
        mask *= 2
    mask = 1
    while mask < lax.axis_size("tok"):
        peak = jnp.maximum(peak, swap(peak, "tok", mask))
        mask *= 2
    return peak


def local(acts, out_grad, kept_ids, cand_ids):
    owners = lax.axis_size("blk")
    toks = lax.axis_size("tok")
    me = lax.axis_index("blk")
    tok = lax.axis_index("tok")
    pos = jnp.stack([me, tok]).astype(jnp.int32)
    ncols = out_grad.shape[1] // BLOCK
    ks = kept_ids.shape[1]
    cs = cand_ids.shape[1]
    kept_share, cand_share = ks // toks, cs // toks
    ids = jnp.concatenate([kept_ids, cand_ids], axis=1)
    cols = ids % ncols
    rows = lax.dynamic_index_in_dim(ids, me, 0, keepdims=False) // ncols

    acts_t = transpose_acts(acts)
    half = cand_share // 2
    bounds = [(0, half), (half, cand_share)]
    cand_chunks = [
        [ks + unit * cand_share + k for unit in range(toks) for k in range(lo, hi)]
        for lo, hi in bounds
    ]
    chunks = cand_chunks + [list(range(ks))]
    gathered = gather_columns(out_grad, cols, pos, owners, chunks)

    pieces = [None] * owners
    pieces[0] = acts_t
    for peer in range(2, owners, 2):
        pieces[peer] = swap(acts_t, "blk", peer)
    for peer in range(0, owners, 2):
        pieces[peer + 1] = swap(pieces[peer], "blk", 1)

    incoming = []
    for which in range(len(chunks)):
        mine = gathered[which * owners : (which + 1) * owners]
        incoming.append([mine[0]] + [swap(mine[p], "blk", p) for p in range(1, owners)])

    cand_parts = []
    for which, (lo, hi) in enumerate(bounds):
        first = lambda unit, lo=lo: ks + unit * cand_share + lo
        part = products(
            pieces, incoming[which], rows, pos, toks, hi - lo, first, jnp.bfloat16
        )
        cand_parts.append([part[0]] + [swap(part[p], "tok", p) for p in range(1, toks)])
    part = products(
        pieces,
        incoming[-1],
        rows,
        pos,
        toks,
        kept_share,
        lambda unit: unit * kept_share,
        jnp.float32,
    )
    kept_parts = [part[0]] + [swap(part[p], "tok", p) for p in range(1, toks)]

    norms, peak = block_norms(cand_parts, [hi - lo for lo, hi in bounds])
    peak = global_peak(peak)
    cand_score = (norms[:cand_share, 0] / (peak[0, 0] + 1e-06))[None]
    kept_grad = kept_sum(kept_parts)
    return (kept_grad, cand_score)


def solution(mesh):
    return jax.shard_map(
        local,
        mesh=mesh,
        in_specs=(P("tok", "blk"), P(("tok", "blk"), None), P(), P()),
        out_specs=(P("blk", "tok", None, None), P("blk", "tok")),
        check_vma=False,
    )
```

time: 320 us -> 131 us (0.41)
  blocking collectives: 115 us -> 0 us
  starting transfers between devices: 5.25 us -> 65.1 us
  waiting for transfers between devices: 98.5 us -> 52.4 us
  local copies, waits for them, and re-layouts: 42.6 us -> 3.59 us
  other arithmetic: 37.6 us -> 0.83 us
  between operations: 14.9 us -> 1.54 us
  Pallas kernels: 0 us -> 7.17 us
  matrix products: 5.71 us -> 0 us
    psum x1 -> x0, blocking collectives: 75.6 us -> none  [local(): kept_full, cand_full = lax.psum((kept_part, cand_part), 'tok')]
    psum x1 -> x0, waiting for transfers between devices: 75.1 us -> none  [local(): kept_full, cand_full = lax.psum((kept_part, cand_part), 'tok')]
    ppermute x0 -> x42, starting transfers between devices: none -> 65.1 us  [swap(): return lax.ppermute(x, axis, [(i, i ^ mask) for i in range(size)])]
    ppermute x0 -> x42, waiting for transfers between devices: none -> 52.4 us  [swap(): return lax.ppermute(x, axis, [(i, i ^ mask) for i in range(size)])]
    pmax x1 -> x0, blocking collectives: 39.4 us -> none  [local(): peak = lax.pmax(jnp.max(norms), ('tok', 'blk'))]
    gather x18 -> x0, local copies, waits for them, and re-layouts: 27.6 us -> none  [the longest x4 8.96 us: one_group(): left = jnp.take(acts3, rows_here, axis=1)]
    all_to_all x1 -> x0, waiting for transfers between devices: 23.4 us -> none  [local(): lax.all_to_all(outgoing, 'blk', split_axis=1, concat_axis=0, tiled=True)]
    scatter-add x1 -> x0, other arithmetic: 22.3 us -> none  [column_table(): jnp.unique(cols, size=width, fill_value=0)]
  transfers between devices with their start and end apart: 3 -> 42, of which waited for: 2 -> 14; matrix products, arithmetic and copies ran while one was open for 15% -> 1% of each run, Pallas kernels for 0% -> 3%
where the time goes in v1:
time: 131 us
  starting transfers between devices  65.1 us (50%)
  waiting for transfers between devices  52.4 us (40%)
  Pallas kernels  7.17 us (5%)
  local copies, waits for them, and re-layouts  3.59 us (3%)
  between operations  1.54 us (1%)
    ppermute x42, starting transfers between devices, swap(): return lax.ppermute(x, axis, [(i, i ^ mask) for i in range(size)])  65.1 us
    ppermute x42, waiting for transfers between devices, swap(): return lax.ppermute(x, axis, [(i, i ^ mask) for i in range(size)])  52.4 us
    pallas_call x3, Pallas kernels, products(): pl.pallas_call(functools.partial(product_kernel, owners, len(grads), toks...  3.93 us
    unnamed x32, local copies, waits for them, and re-layouts  3.08 us
  transfers between devices with their start and end apart: 42, of which 14 were waited for; matrix products, arithmetic and copies ran while one was open for 1% of the time, Pallas kernels for 3%

profile of v1, /device:TPU:0, one launch (start us, length us, event | category | flops | bytes accessed | tf_op | source)
XLA Modules:
  0.0 130.7 jit_solution(2368023867221826350)
XLA Ops:
  2.6 2.1 %shard_map.60 = (bf16[24,16,128]{2,1,0:T(8,128)(2,1)S(1)}, bf16[24,16,128]{2,1,0:T(8,128)(2,1)S(1)}, bf16[24,16,128]{2,1,0:T(8,128)(2,1)S(1)}, bf16[24,16,128]{2...) custom-call(s32[2]{0:T(128)S(1)} %pad_add_fusion.1.pos, ...), custom_call_target="tpu_custom_call" | custom-call | tf_op jit(solution)/shard_map/pallas_call | solution.py:61
  6.6 2.9 %collective-permute-start.8 = (bf16[16,16,128]{2,1,0:T(8,128)(2,1)S(1)}, bf16[16,16,128]{2,1,0:T(8,128)(2,1)S(1)}, u32[]{:S(2)}, u32[]{:S(2)}) collective-permute-start(bf16[16,16,128]{2,1,0:T(8,128)(2,1)S(1)} %get-tuple-element.42), channel_id=1, source_target_pairs={{0,2},{1,3},{2,0},{3,1},{4,6},{5,7},{6,4},{7,5},{8,10},{9,11},{10,... | collective-permute-start | bytes 196616 | tf_op jit(solution)/shard_map/ppermute | solution.py:20
  9.7 2.1 %collective-permute-start.1 = (bf16[1024,128]{1,0:T(8,128)(2,1)S(1)}, bf16[1024,128]{1,0:T(8,128)(2,1)S(1)}, u32[]{:S(2)}, u32[]{:S(2)}) collective-permute-start(bf16[1024,128]{1,0:T(8,128)(2,1)S(1)} %shard_map.59.refs_0_), channel_id=1, source_target_pairs={{0,2},{1,3},{2,0},{3,1},{4,6},{5,7},{6,4},{7,5},{8,10},{9,11},{10,... | collective-permute-start | bytes 786440 | tf_op jit(solution)/shard_map/ppermute | solution.py:20
  13.3 2.1 %collective-permute-start.5 = (bf16[1024,128]{1,0:T(8,128)(2,1)S(1)}, bf16[1024,128]{1,0:T(8,128)(2,1)S(1)}, u32[]{:S(2)}, u32[]{:S(2)}) collective-permute-start(bf16[1024,128]{1,0:T(8,128)(2,1)S(1)} %shard_map.59.refs_0_), channel_id=1, source_target_pairs={{0,6},{1,7},{2,4},{3,5},{4,2},{5,3},{6,0},{7,1},{8,14},{9,15},{10,... | collective-permute-start | bytes 786440 | tf_op jit(solution)/shard_map/ppermute | solution.py:20
  16.7 9.9 %collective-permute-done.19.refs_11_ = bf16[24,16,128]{2,1,0:T(8,128)(2,1)S(1)} collective-permute-done((bf16[24,16,128]{2,1,0:T(8,128)(2,1)S(1)}, bf16[24,16,128]{2,1,0:T(8,128)(2,1)S(1)}, u32[]{:S(2)}, u32[]{:S(2)}) %collective-permute-start.19) | collective-permute-done | bytes 98336 | tf_op jit(solution)/shard_map/ppermute | solution.py:20
  26.6 2.1 %collective-permute-start.21 = (bf16[24,16,128]{2,1,0:T(8,128)(2,1)S(1)}, bf16[24,16,128]{2,1,0:T(8,128)(2,1)S(1)}, u32[]{:S(2)}, u32[]{:S(2)}) collective-permute-start(bf16[24,16,128]{2,1,0:T(8,128)(2,1)S(1)} %get-tuple-element.57), channel_id=1, source_target_pairs={{0,5},{1,4},{2,7},{3,6},{4,1},{5,0},{6,3},{7,2},{8,13},{9,12},{10,... | collective-permute-start | bytes 294920 | tf_op jit(solution)/shard_map/ppermute | solution.py:20
  29.9 3.2 %collective-permute-done.21.refs_13_ = bf16[24,16,128]{2,1,0:T(8,128)(2,1)S(1)} collective-permute-done((bf16[24,16,128]{2,1,0:T(8,128)(2,1)S(1)}, bf16[24,16,128]{2,1,0:T(8,128)(2,1)S(1)}, u32[]{:S(2)}, u32[]{:S(2)}) %collective-permute-start.21) | collective-permute-done | bytes 98336 | tf_op jit(solution)/shard_map/ppermute | solution.py:20
  33.2 2.5 %collective-permute-start.23 = (bf16[24,16,128]{2,1,0:T(8,128)(2,1)S(1)}, bf16[24,16,128]{2,1,0:T(8,128)(2,1)S(1)}, u32[]{:S(2)}, u32[]{:S(2)}) collective-permute-start(bf16[24,16,128]{2,1,0:T(8,128)(2,1)S(1)} %get-tuple-element.59), channel_id=1, source_target_pairs={{0,7},{1,6},{2,5},{3,4},{4,3},{5,2},{6,1},{7,0},{8,15},{9,14},{10,... | collective-permute-start | bytes 294920 | tf_op jit(solution)/shard_map/ppermute | solution.py:20
  39.4 1.9 %collective-permute-start.28 = (bf16[24,16,128]{2,1,0:T(8,128)(2,1)}, bf16[24,16,128]{2,1,0:T(8,128)(2,1)S(1)}, u32[]{:S(2)}, u32[]{:S(2)}) collective-permute-start(bf16[24,16,128]{2,1,0:T(8,128)(2,1)} %get-tuple-element.66), channel_id=1, source_target_pairs={{0,2},{1,3},{2,0},{3,1},{4,6},{5,7},{6,4},{7,5},{8,10},{9,11},{10,... | collective-permute-start | bytes 294920 | tf_op jit(solution)/shard_map/ppermute | solution.py:20
  41.3 3.3 %collective-permute-done.28.refs_10_ = bf16[24,16,128]{2,1,0:T(8,128)(2,1)S(1)} collective-permute-done((bf16[24,16,128]{2,1,0:T(8,128)(2,1)}, bf16[24,16,128]{2,1,0:T(8,128)(2,1)S(1)}, u32[]{:S(2)}, u32[]{:S(2)}) %collective-permute-start.28) | collective-permute-done | bytes 98336 | tf_op jit(solution)/shard_map/ppermute | solution.py:20
  45.3 1.7 %collective-permute-start.30 = (bf16[24,16,128]{2,1,0:T(8,128)(2,1)}, bf16[24,16,128]{2,1,0:T(8,128)(2,1)S(1)}, u32[]{:S(2)}, u32[]{:S(2)}) collective-permute-start(bf16[24,16,128]{2,1,0:T(8,128)(2,1)} %copy-done.4), channel_id=1, source_target_pairs={{0,4},{1,5},{2,6},{3,7},{4,0},{5,1},{6,2},{7,3},{8,12},{9,13},{10,... | collective-permute-start | bytes 294920 | tf_op jit(solution)/shard_map/ppermute | solution.py:20
  47.8 2.0 %collective-permute-start.32 = (bf16[24,16,128]{2,1,0:T(8,128)(2,1)}, bf16[24,16,128]{2,1,0:T(8,128)(2,1)S(1)}, u32[]{:S(2)}, u32[]{:S(2)}) collective-permute-start(bf16[24,16,128]{2,1,0:T(8,128)(2,1)} %copy-done.2), channel_id=1, source_target_pairs={{0,6},{1,7},{2,4},{3,5},{4,2},{5,3},{6,0},{7,1},{8,14},{9,15},{10,... | collective-permute-start | bytes 294920 | tf_op jit(solution)/shard_map/ppermute | solution.py:20
  54.2 3.3 %collective-permute-done.31.refs_13_ = bf16[24,16,128]{2,1,0:T(8,128)(2,1)S(1)} collective-permute-done((bf16[24,16,128]{2,1,0:T(8,128)(2,1)}, bf16[24,16,128]{2,1,0:T(8,128)(2,1)S(1)}, u32[]{:S(2)}, u32[]{:S(2)}) %collective-permute-start.31) | collective-permute-done | bytes 98336 | tf_op jit(solution)/shard_map/ppermute | solution.py:20
  59.2 2.0 %collective-permute-start.12 = (bf16[16,16,128]{2,1,0:T(8,128)(2,1)S(1)}, bf16[16,16,128]{2,1,0:T(8,128)(2,1)S(1)}, u32[]{:S(2)}, u32[]{:S(2)}) collective-permute-start(bf16[16,16,128]{2,1,0:T(8,128)(2,1)S(1)} %copy-done.7), channel_id=1, source_target_pairs={{0,6},{1,7},{2,4},{3,5},{4,2},{5,3},{6,0},{7,1},{8,14},{9,15},{10,... | collective-permute-start | bytes 196616 | tf_op jit(solution)/shard_map/ppermute | solution.py:20
  62.6 2.7 %collective-permute-start.25 = (bf16[6,128,128]{2,1,0:T(8,128)(2,1)S(1)}, bf16[6,128,128]{2,1,0:T(8,128)(2,1)S(1)}, u32[]{:S(2)}, u32[]{:S(2)}) collective-permute-start(bf16[6,128,128]{2,1,0:T(8,128)(2,1)S(1)} %get-tuple-element.62), channel_id=1, source_target_pairs={{0,16},{8,24},{16,0},{24,8},{1,17},{9,25},{17,1},{25,9},{2,18},{10... | collective-permute-start | bytes 589832 | tf_op jit(solution)/shard_map/ppermute | solution.py:20
  67.0 5.1 %collective-permute-done.13.refs_15_ = bf16[16,16,128]{2,1,0:T(8,128)(2,1)S(1)} collective-permute-done((bf16[16,16,128]{2,1,0:T(8,128)(2,1)S(1)}, bf16[16,16,128]{2,1,0:T(8,128)(2,1)S(1)}, u32[]{:S(2)}, u32[]{:S(2)}) %collective-permute-start.13) | collective-permute-done | bytes 65568 | tf_op jit(solution)/shard_map/ppermute | solution.py:20
  72.1 2.6 %collective-permute-start.35 = (bf16[6,128,128]{2,1,0:T(8,128)(2,1)S(1)}, bf16[6,128,128]{2,1,0:T(8,128)(2,1)S(1)}, u32[]{:S(2)}, u32[]{:S(2)}) collective-permute-start(bf16[6,128,128]{2,1,0:T(8,128)(2,1)S(1)} %get-tuple-element.74), channel_id=1, source_target_pairs={{0,16},{8,24},{16,0},{24,8},{1,17},{9,25},{17,1},{25,9},{2,18},{10... | collective-permute-start | bytes 589832 | tf_op jit(solution)/shard_map/ppermute | solution.py:20
  77.3 2.4 %collective-permute-done.25.refs_2_ = bf16[6,128,128]{2,1,0:T(8,128)(2,1)S(1)} collective-permute-done((bf16[6,128,128]{2,1,0:T(8,128)(2,1)S(1)}, bf16[6,128,128]{2,1,0:T(8,128)(2,1)S(1)}, u32[]{:S(2)}, u32[]{:S(2)}) %collective-permute-start.25) | collective-permute-done | bytes 196640 | tf_op jit(solution)/shard_map/ppermute | solution.py:20
  80.2 14.3 %collective-permute-start.15 = (f32[4,128,128]{2,1,0:T(8,128)S(1)}, f32[4,128,128]{2,1,0:T(8,128)S(1)}, u32[]{:S(2)}, u32[]{:S(2)}) collective-permute-start(f32[4,128,128]{2,1,0:T(8,128)S(1)} %get-tuple-element.50), channel_id=1, source_target_pairs={{0,16},{8,24},{16,0},{24,8},{1,17},{9,25},{17,1},{25,9},{2,18},{10... | collective-permute-start | bytes 786440 | tf_op jit(solution)/shard_map/ppermute | solution.py:20
  95.3 12.5 %collective-permute-done.35.refs_6_ = bf16[6,128,128]{2,1,0:T(8,128)(2,1)S(1)} collective-permute-done((bf16[6,128,128]{2,1,0:T(8,128)(2,1)S(1)}, bf16[6,128,128]{2,1,0:T(8,128)(2,1)S(1)}, u32[]{:S(2)}, u32[]{:S(2)}) %collective-permute-start.35) | collective-permute-done | bytes 196640 | tf_op jit(solution)/shard_map/ppermute | solution.py:20
  110.2 2.7 %collective-permute-done.38 = f32[8,128]{1,0:T(8,128)S(1)} collective-permute-done((f32[8,128]{1,0:T(8,128)S(1)}, f32[8,128]{1,0:T(8,128)S(1)}, u32[]{:S(2)}, u32[]{:S(2)}) %collective-permute-start.38) | collective-permute-done | bytes 4128 | tf_op jit(solution)/shard_map/ppermute | solution.py:20
  113.6 2.9 %collective-permute-done.39 = f32[8,128]{1,0:T(8,128)S(1)} collective-permute-done((f32[8,128]{1,0:T(8,128)S(1)}, f32[8,128]{1,0:T(8,128)S(1)}, u32[]{:S(2)}, u32[]{:S(2)}) %collective-permute-start.39) | collective-permute-done | bytes 4128 | tf_op jit(solution)/shard_map/ppermute | solution.py:20
  116.5 4.8 %collective-permute-start.40 = (f32[8,128]{1,0:T(8,128)S(1)}, f32[8,128]{1,0:T(8,128)S(1)}, u32[]{:S(2)}, u32[]{:S(2)}) collective-permute-start(f32[8,128]{1,0:T(8,128)S(1)} %max.17), channel_id=1, source_target_pairs={{0,8},{8,0},{16,24},{24,16},{1,9},{9,1},{17,25},{25,17},{2,10},{10... | collective-permute-start | bytes 12296 | tf_op jit(solution)/shard_map/ppermute | solution.py:20
  122.9 3.7 %collective-permute-start.41 = (f32[8,128]{1,0:T(8,128)S(1)}, f32[8,128]{1,0:T(8,128)S(1)}, u32[]{:S(2)}, u32[]{:S(2)}) collective-permute-start(f32[8,128]{1,0:T(8,128)S(1)} %max.18), channel_id=1, source_target_pairs={{0,16},{8,24},{16,0},{24,8},{1,17},{9,25},{17,1},{25,9},{2,18},{10... | collective-permute-start | bytes 12296 | tf_op jit(solution)/shard_map/ppermute | solution.py:20
  (109 shorter events, 34.5 us)
Async XLA Ops:
  6.0 9.4 %collective-permute-start.17 = (bf16[24,16,128]{2,1,0:T(8,128)(2,1)S(1)}, bf16[24,16,128]{2,1,0:T(8,128)(2,1)S(1)}, u32[]{:S(2)}, u32[]{:S(2)}) collective-permute-start(bf16[24,16,128]{2,1,0:T(8,128)(2,1)S(1)} %get-tuple-element.53), channel_id=1, source_target_pairs={{0,1},{1,0},{2,3},{3,2},{4,5},{5,4},{6,7},{7,6},{8,9},{9,8},{10,11... | collective-permute-start | bytes 294920 | tf_op jit(solution)/shard_map/ppermute | solution.py:20
  9.7 26.0 %collective-permute-start.1 = (bf16[1024,128]{1,0:T(8,128)(2,1)S(1)}, bf16[1024,128]{1,0:T(8,128)(2,1)S(1)}, u32[]{:S(2)}, u32[]{:S(2)}) collective-permute-start(bf16[1024,128]{1,0:T(8,128)(2,1)S(1)} %shard_map.59.refs_0_), channel_id=1, source_target_pairs={{0,2},{1,3},{2,0},{3,1},{4,6},{5,7},{6,4},{7,5},{8,10},{9,11},{10,... | collective-permute-start | bytes 786440 | tf_op jit(solution)/shard_map/ppermute | solution.py:20
  11.8 24.5 %collective-permute-start.3 = (bf16[1024,128]{1,0:T(8,128)(2,1)S(1)}, bf16[1024,128]{1,0:T(8,128)(2,1)S(1)}, u32[]{:S(2)}, u32[]{:S(2)}) collective-permute-start(bf16[1024,128]{1,0:T(8,128)(2,1)S(1)} %shard_map.59.refs_0_), channel_id=1, source_target_pairs={{0,4},{1,5},{2,6},{3,7},{4,0},{5,1},{6,2},{7,3},{8,12},{9,13},{10,... | collective-permute-start | bytes 786440 | tf_op jit(solution)/shard_map/ppermute | solution.py:20
  13.3 23.0 %collective-permute-start.5 = (bf16[1024,128]{1,0:T(8,128)(2,1)S(1)}, bf16[1024,128]{1,0:T(8,128)(2,1)S(1)}, u32[]{:S(2)}, u32[]{:S(2)}) collective-permute-start(bf16[1024,128]{1,0:T(8,128)(2,1)S(1)} %shard_map.59.refs_0_), channel_id=1, source_target_pairs={{0,6},{1,7},{2,4},{3,5},{4,2},{5,3},{6,0},{7,1},{8,14},{9,15},{10,... | collective-permute-start | bytes 786440 | tf_op jit(solution)/shard_map/ppermute | solution.py:20
  15.4 11.2 %collective-permute-start.19 = (bf16[24,16,128]{2,1,0:T(8,128)(2,1)S(1)}, bf16[24,16,128]{2,1,0:T(8,128)(2,1)S(1)}, u32[]{:S(2)}, u32[]{:S(2)}) collective-permute-start(bf16[24,16,128]{2,1,0:T(8,128)(2,1)S(1)} %get-tuple-element.55), channel_id=1, source_target_pairs={{0,3},{1,2},{2,1},{3,0},{4,7},{5,6},{6,5},{7,4},{8,11},{9,10},{10,... | collective-permute-start | bytes 294920 | tf_op jit(solution)/shard_map/ppermute | solution.py:20
  15.4 13.3 %collective-permute-start.20 = (bf16[24,16,128]{2,1,0:T(8,128)(2,1)S(1)}, bf16[24,16,128]{2,1,0:T(8,128)(2,1)S(1)}, u32[]{:S(2)}, u32[]{:S(2)}) collective-permute-start(bf16[24,16,128]{2,1,0:T(8,128)(2,1)S(1)} %get-tuple-element.56), channel_id=1, source_target_pairs={{0,4},{1,5},{2,6},{3,7},{4,0},{5,1},{6,2},{7,3},{8,12},{9,13},{10,... | collective-permute-start | bytes 294920 | tf_op jit(solution)/shard_map/ppermute | solution.py:20
  35.7 9.6 %collective-permute-start = (bf16[1024,128]{1,0:T(8,128)(2,1)S(1)}, bf16[1024,128]{1,0:T(8,128)(2,1)S(1)}, u32[]{:S(2)}, u32[]{:S(2)}) collective-permute-start(bf16[1024,128]{1,0:T(8,128)(2,1)S(1)} %shard_map.59.refs_0_), channel_id=1, source_target_pairs={{0,1},{1,0},{2,3},{3,2},{4,5},{5,4},{6,7},{7,6},{8,9},{9,8},{10,11... | collective-permute-start | bytes 786440 | tf_op jit(solution)/shard_map/ppermute | solution.py:20
  35.7 11.3 %collective-permute-start.2 = (bf16[1024,128]{1,0:T(8,128)(2,1)S(1)}, bf16[1024,128]{1,0:T(8,128)(2,1)S(1)}, u32[]{:S(2)}, u32[]{:S(2)}) collective-permute-start(bf16[1024,128]{1,0:T(8,128)(2,1)S(1)} %collective-permute-done.1.refs_2_), channel_id=1, source_target_pairs={{0,1},{1,0},{2,3},{3,2},{4,5},{5,4},{6,7},{7,6},{8,9},{9,8},{10,11... | collective-permute-start | bytes 786440 | tf_op jit(solution)/shard_map/ppermute | solution.py:20
  36.2 11.6 %collective-permute-start.4 = (bf16[1024,128]{1,0:T(8,128)(2,1)S(1)}, bf16[1024,128]{1,0:T(8,128)(2,1)S(1)}, u32[]{:S(2)}, u32[]{:S(2)}) collective-permute-start(bf16[1024,128]{1,0:T(8,128)(2,1)S(1)} %collective-permute-done.3.refs_4_), channel_id=1, source_target_pairs={{0,1},{1,0},{2,3},{3,2},{4,5},{5,4},{6,7},{7,6},{8,9},{9,8},{10,11... | collective-permute-start | bytes 786440 | tf_op jit(solution)/shard_map/ppermute | solution.py:20
  36.3 13.5 %collective-permute-start.6 = (bf16[1024,128]{1,0:T(8,128)(2,1)S(1)}, bf16[1024,128]{1,0:T(8,128)(2,1)S(1)}, u32[]{:S(2)}, u32[]{:S(2)}) collective-permute-start(bf16[1024,128]{1,0:T(8,128)(2,1)S(1)} %collective-permute-done.5.refs_6_), channel_id=1, source_target_pairs={{0,1},{1,0},{2,3},{3,2},{4,5},{5,4},{6,7},{7,6},{8,9},{9,8},{10,11... | collective-permute-start | bytes 786440 | tf_op jit(solution)/shard_map/ppermute | solution.py:20
  45.3 7.8 %collective-permute-start.30 = (bf16[24,16,128]{2,1,0:T(8,128)(2,1)}, bf16[24,16,128]{2,1,0:T(8,128)(2,1)S(1)}, u32[]{:S(2)}, u32[]{:S(2)}) collective-permute-start(bf16[24,16,128]{2,1,0:T(8,128)(2,1)} %copy-done.4), channel_id=1, source_target_pairs={{0,4},{1,5},{2,6},{3,7},{4,0},{5,1},{6,2},{7,3},{8,12},{9,13},{10,... | collective-permute-start | bytes 294920 | tf_op jit(solution)/shard_map/ppermute | solution.py:20
  47.0 10.5 %collective-permute-start.31 = (bf16[24,16,128]{2,1,0:T(8,128)(2,1)}, bf16[24,16,128]{2,1,0:T(8,128)(2,1)S(1)}, u32[]{:S(2)}, u32[]{:S(2)}) collective-permute-start(bf16[24,16,128]{2,1,0:T(8,128)(2,1)} %copy-done.3), channel_id=1, source_target_pairs={{0,5},{1,4},{2,7},{3,6},{4,1},{5,0},{6,3},{7,2},{8,13},{9,12},{10,... | collective-permute-start | bytes 294920 | tf_op jit(solution)/shard_map/ppermute | solution.py:20
  47.8 11.4 %collective-permute-start.32 = (bf16[24,16,128]{2,1,0:T(8,128)(2,1)}, bf16[24,16,128]{2,1,0:T(8,128)(2,1)S(1)}, u32[]{:S(2)}, u32[]{:S(2)}) collective-permute-start(bf16[24,16,128]{2,1,0:T(8,128)(2,1)} %copy-done.2), channel_id=1, source_target_pairs={{0,6},{1,7},{2,4},{3,5},{4,2},{5,3},{6,0},{7,1},{8,14},{9,15},{10,... | collective-permute-start | bytes 294920 | tf_op jit(solution)/shard_map/ppermute | solution.py:20
  49.9 9.3 %collective-permute-start.33 = (bf16[24,16,128]{2,1,0:T(8,128)(2,1)S(1)}, bf16[24,16,128]{2,1,0:T(8,128)(2,1)S(1)}, u32[]{:S(2)}, u32[]{:S(2)}) collective-permute-start(bf16[24,16,128]{2,1,0:T(8,128)(2,1)S(1)} %get-tuple-element.71), channel_id=1, source_target_pairs={{0,7},{1,6},{2,5},{3,4},{4,3},{5,2},{6,1},{7,0},{8,15},{9,14},{10,... | collective-permute-start | bytes 294920 | tf_op jit(solution)/shard_map/ppermute | solution.py:20
  51.4 23.2 %collective-permute-start.24 = (bf16[6,128,128]{2,1,0:T(8,128)(2,1)S(1)}, bf16[6,128,128]{2,1,0:T(8,128)(2,1)S(1)}, u32[]{:S(2)}, u32[]{:S(2)}) collective-permute-start(bf16[6,128,128]{2,1,0:T(8,128)(2,1)S(1)} %get-tuple-element.61), channel_id=1, source_target_pairs={{0,8},{8,0},{16,24},{24,16},{1,9},{9,1},{17,25},{25,17},{2,10},{10... | collective-permute-start | bytes 589832 | tf_op jit(solution)/shard_map/ppermute | solution.py:20
  53.1 9.5 %collective-permute-start.9 = (bf16[16,16,128]{2,1,0:T(8,128)(2,1)S(1)}, bf16[16,16,128]{2,1,0:T(8,128)(2,1)S(1)}, u32[]{:S(2)}, u32[]{:S(2)}) collective-permute-start(bf16[16,16,128]{2,1,0:T(8,128)(2,1)S(1)} %copy-done.13), channel_id=1, source_target_pairs={{0,3},{1,2},{2,1},{3,0},{4,7},{5,6},{6,5},{7,4},{8,11},{9,10},{10,... | collective-permute-start | bytes 196616 | tf_op jit(solution)/shard_map/ppermute | solution.py:20
  62.6 17.1 %collective-permute-start.25 = (bf16[6,128,128]{2,1,0:T(8,128)(2,1)S(1)}, bf16[6,128,128]{2,1,0:T(8,128)(2,1)S(1)}, u32[]{:S(2)}, u32[]{:S(2)}) collective-permute-start(bf16[6,128,128]{2,1,0:T(8,128)(2,1)S(1)} %get-tuple-element.62), channel_id=1, source_target_pairs={{0,16},{8,24},{16,0},{24,8},{1,17},{9,25},{17,1},{25,9},{2,18},{10... | collective-permute-start | bytes 589832 | tf_op jit(solution)/shard_map/ppermute | solution.py:20
  65.2 15.0 %collective-permute-start.26 = (bf16[6,128,128]{2,1,0:T(8,128)(2,1)S(1)}, bf16[6,128,128]{2,1,0:T(8,128)(2,1)S(1)}, u32[]{:S(2)}, u32[]{:S(2)}) collective-permute-start(bf16[6,128,128]{2,1,0:T(8,128)(2,1)S(1)} %get-tuple-element.63), channel_id=1, source_target_pairs={{0,24},{8,16},{16,8},{24,0},{1,25},{9,17},{17,9},{25,1},{2,26},{10... | collective-permute-start | bytes 589832 | tf_op jit(solution)/shard_map/ppermute | solution.py:20
  66.6 27.9 %collective-permute-start.34 = (bf16[6,128,128]{2,1,0:T(8,128)(2,1)S(1)}, bf16[6,128,128]{2,1,0:T(8,128)(2,1)S(1)}, u32[]{:S(2)}, u32[]{:S(2)}) collective-permute-start(bf16[6,128,128]{2,1,0:T(8,128)(2,1)S(1)} %get-tuple-element.73), channel_id=1, source_target_pairs={{0,8},{8,0},{16,24},{24,16},{1,9},{9,1},{17,25},{25,17},{2,10},{10... | collective-permute-start | bytes 589832 | tf_op jit(solution)/shard_map/ppermute | solution.py:20
  72.1 35.7 %collective-permute-start.35 = (bf16[6,128,128]{2,1,0:T(8,128)(2,1)S(1)}, bf16[6,128,128]{2,1,0:T(8,128)(2,1)S(1)}, u32[]{:S(2)}, u32[]{:S(2)}) collective-permute-start(bf16[6,128,128]{2,1,0:T(8,128)(2,1)S(1)} %get-tuple-element.74), channel_id=1, source_target_pairs={{0,16},{8,24},{16,0},{24,8},{1,17},{9,25},{17,1},{25,9},{2,18},{10... | collective-permute-start | bytes 589832 | tf_op jit(solution)/shard_map/ppermute | solution.py:20
  74.7 33.1 %collective-permute-start.36 = (bf16[6,128,128]{2,1,0:T(8,128)(2,1)S(1)}, bf16[6,128,128]{2,1,0:T(8,128)(2,1)S(1)}, u32[]{:S(2)}, u32[]{:S(2)}) collective-permute-start(bf16[6,128,128]{2,1,0:T(8,128)(2,1)S(1)} %get-tuple-element.75), channel_id=1, source_target_pairs={{0,24},{8,16},{16,8},{24,0},{1,25},{9,17},{17,9},{25,1},{2,26},{10... | collective-permute-start | bytes 589832 | tf_op jit(solution)/shard_map/ppermute | solution.py:20
  79.7 50.2 %collective-permute-start.14 = (f32[4,128,128]{2,1,0:T(8,128)S(1)}, f32[4,128,128]{2,1,0:T(8,128)S(1)}, u32[]{:S(2)}, u32[]{:S(2)}) collective-permute-start(f32[4,128,128]{2,1,0:T(8,128)S(1)} %get-tuple-element.49), channel_id=1, source_target_pairs={{0,8},{8,0},{16,24},{24,16},{1,9},{9,1},{17,25},{25,17},{2,10},{10... | collective-permute-start | bytes 786440 | tf_op jit(solution)/shard_map/ppermute | solution.py:20
  80.2 49.7 %collective-permute-start.15 = (f32[4,128,128]{2,1,0:T(8,128)S(1)}, f32[4,128,128]{2,1,0:T(8,128)S(1)}, u32[]{:S(2)}, u32[]{:S(2)}) collective-permute-start(f32[4,128,128]{2,1,0:T(8,128)S(1)} %get-tuple-element.50), channel_id=1, source_target_pairs={{0,16},{8,24},{16,0},{24,8},{1,17},{9,25},{17,1},{25,9},{2,18},{10... | collective-permute-start | bytes 786440 | tf_op jit(solution)/shard_map/ppermute | solution.py:20
  94.5 35.4 %collective-permute-start.16 = (f32[4,128,128]{2,1,0:T(8,128)S(1)}, f32[4,128,128]{2,1,0:T(8,128)S(1)}, u32[]{:S(2)}, u32[]{:S(2)}) collective-permute-start(f32[4,128,128]{2,1,0:T(8,128)S(1)} %get-tuple-element.51), channel_id=1, source_target_pairs={{0,24},{8,16},{16,8},{24,0},{1,25},{9,17},{17,9},{25,1},{2,26},{10... | collective-permute-start | bytes 786440 | tf_op jit(solution)/shard_map/ppermute | solution.py:20
  (34 other events, 159.7 us)

commit v2 on v0

v2 whole, which is shorter than its diff:
```python
import functools

import jax
import jax.numpy as jnp
from jax import lax
from jax.experimental import pallas as pl
from jax.experimental.pallas import tpu as pltpu
from jax.sharding import PartitionSpec as P

BLOCK = 128
ROWS = 16
PER_BLOCK = BLOCK // ROWS
VMEM_LIMIT = 40 * 1024 * 1024
ANY = pl.BlockSpec(memory_space=pl.ANY)
VMEM = pl.BlockSpec(memory_space=pltpu.VMEM)
SMEM = pl.BlockSpec(memory_space=pltpu.SMEM)
PARAMS = pltpu.CompilerParams(vmem_limit_bytes=VMEM_LIMIT)


def swap(x, axis, mask):
    size = lax.axis_size(axis)
    return lax.ppermute(x, axis, [(i, i ^ mask) for i in range(size)])


def call(kernel, outs, args, specs, out_specs, scratch=()):
    return pl.pallas_call(
        kernel,
        out_shape=outs,
        in_specs=specs,
        out_specs=out_specs,
        scratch_shapes=scratch,
        compiler_params=PARAMS,
    )(*args)


def pack_kernel(slots, masks, with_acts, pos, cols, grad, *refs):
    outs = refs[1:] if with_acts else refs
    me = pos[0]
    base = 0
    if with_acts:
        acts = refs[0]
        base = acts.shape[1] // ROWS
        for row in range(acts.shape[1] // BLOCK):
            block = acts[:, row * BLOCK : (row + 1) * BLOCK].T
            block = block.reshape(PER_BLOCK, ROWS, BLOCK)
            for out in outs:
                out[row * PER_BLOCK : (row + 1) * PER_BLOCK] = block
    for out, dests in zip(outs, masks):
        at = base
        for mask in dests:
            dest = me ^ mask
            for slot in slots:
                start = pl.multiple_of(cols[dest, slot] * BLOCK, BLOCK)
                out[at] = grad[:, pl.ds(start, BLOCK)]
                at += 1


def exchange(out_grad, cols, pos, slots, acts=None):
    owners = lax.axis_size("blk")
    masks = [(0,), (1,)] + [(m, m + 1) for m in range(2, owners, 2)]
    base = 0 if acts is None else acts.shape[1] // ROWS
    count = len(slots)
    buffers = call(
        functools.partial(pack_kernel, slots, masks, acts is not None),
        [
            jax.ShapeDtypeStruct((base + len(d) * count, ROWS, BLOCK), out_grad.dtype)
            for d in masks
        ],
        (pos, cols, out_grad) + (() if acts is None else (acts,)),
        [SMEM, SMEM, VMEM] + ([] if acts is None else [VMEM]),
        [VMEM] * len(masks),
    )
    got = [None] * owners
    got[0] = (buffers[0], base)
    for k in range(len(masks) - 1, 1, -1):
        got[2 * k - 2] = (swap(buffers[k], "blk", 2 * k - 2), base)
    got[1] = (swap(buffers[1], "blk", 1), base)
    for mask in range(2, owners, 2):
        got[mask + 1] = (swap(got[mask][0], "blk", 1), base + count)
    return got


def exchange_plain(out_grad, cols, pos, slots, acts=None):
    owners = lax.axis_size("blk")
    rows = out_grad.shape[0]
    count = len(slots)
    grad3 = out_grad.reshape(rows, -1, BLOCK)
    outgoing = jnp.take(grad3, cols[:, jnp.array(slots)].reshape(-1), axis=1)
    outgoing = outgoing.reshape(rows, owners, count, BLOCK).transpose(1, 2, 0, 3)
    incoming = lax.all_to_all(outgoing, "blk", 0, 0, tiled=True)
    grads = jnp.swapaxes(incoming, 0, 1).reshape(count * PER_BLOCK, ROWS, BLOCK)
    if acts is None:
        return [grads]
    whole = lax.all_gather(acts.T, "blk", axis=0, tiled=True)
    return [grads, whole.reshape(-1, ROWS, BLOCK)]


def product_kernel(plan, toks, share, first, pos, rows, *refs):
    copies_of, inputs = plan
    srcs = refs[:inputs]
    keep, send, acts_all, grad_all, sem = refs[inputs:]
    me, tok = pos[0], pos[1]
    copies = []
    for n, (which, src, begin, size, peer) in enumerate(copies_of):
        at = 0 if peer is None else me ^ peer
        from_ref = srcs[src].at[pl.ds(begin, size)]
        if which == "acts":
            dst = acts_all.at[pl.ds(pl.multiple_of(at * size, size), size)]
        elif peer is None:
            dst = grad_all
            from_ref = from_ref.reshape(grad_all.shape)
        else:
            dst = grad_all.at[:, pl.ds(pl.multiple_of(at * ROWS, ROWS), ROWS)]
        copies.append(pltpu.make_async_copy(from_ref, dst, sem.at[n]))
    for copy in copies:
        copy.start()
    for copy in copies:
        copy.wait()
    for peer in range(toks):
        unit = tok ^ peer
        for k in range(share):
            slot = unit * share + k
            row = rows[first(unit) + k] * PER_BLOCK
            left = acts_all[pl.ds(pl.multiple_of(row, PER_BLOCK), PER_BLOCK)]
            prod = jnp.dot(
                left.reshape(BLOCK, BLOCK), grad_all[slot], preferred_element_type=jnp.float32
            )
            out = send if peer % 2 else keep
            out[(peer // 2) * share + k] = prod.astype(out.dtype)


def products(acts_from, grads_from, width, rows, pos, toks, share, first, dtype):
    owners = lax.axis_size("blk")
    count = toks * share
    buffers = []
    copies = []

    def index(buffer):
        for n, other in enumerate(buffers):
            if other is buffer:
                return n
        buffers.append(buffer)
        return len(buffers) - 1

    if isinstance(acts_from[0], tuple):
        for peer in range(owners):
            copies.append(("acts", index(acts_from[peer][0]), 0, width, peer))
            buffer, begin = grads_from[peer]
            copies.append(("grad", index(buffer), begin, count, peer))
    else:
        whole = acts_from[1]
        copies.append(("acts", index(whole), 0, whole.shape[0], None))
        grads = grads_from[0]
        copies.append(("grad", index(grads), 0, grads.shape[0], None))
    units = toks // 2 * share
    return call(
        functools.partial(product_kernel, (copies, len(buffers)), toks, share, first),
        [
            jax.ShapeDtypeStruct((units, BLOCK, BLOCK), jnp.float32),
            jax.ShapeDtypeStruct((units, BLOCK, BLOCK), dtype),
        ],
        [pos, rows] + buffers,
        [SMEM, SMEM] + [ANY] * len(buffers),
        [VMEM] * 2,
        [
            pltpu.VMEM((owners * width, ROWS, BLOCK), jnp.bfloat16),
            pltpu.VMEM((count, BLOCK, BLOCK), jnp.bfloat16),
            pltpu.SemaphoreType.DMA((len(copies),)),
        ],
    )


def add_kernel(share, keep, got, keep_out, send_out):
    for k in range(keep.shape[0]):
        unit, part = divmod(k, share)
        total = keep[k] + got[k].astype(jnp.float32)
        out = send_out if unit % 2 else keep_out
        out[(unit // 2) * share + part] = total.astype(out.dtype)


def halve(keep, send, share):
    toks = lax.axis_size("tok")
    mask = 1
    got = swap(send, "tok", mask)
    while 2 * mask < toks:
        mask *= 2
        half = keep.shape[0] // 2
        keep, send = call(
            functools.partial(add_kernel, share),
            [
                jax.ShapeDtypeStruct((half, BLOCK, BLOCK), jnp.float32),
                jax.ShapeDtypeStruct((half, BLOCK, BLOCK), send.dtype),
            ],
            (keep, got),
            [VMEM] * 2,
            [VMEM] * 2,
        )
        got = swap(send, "tok", mask)
    return keep, got


def norm_kernel(*refs):
    row_out, peak_out = refs[-2:]
    lane = lax.broadcasted_iota(jnp.int32, row_out.shape, 1)
    row = jnp.zeros(row_out.shape, jnp.float32)
    at = 0
    for keep, got in zip(refs[:-2:2], refs[1:-2:2]):
        for k in range(keep.shape[0]):
            total = keep[k] + got[k].astype(jnp.float32)
            square = jnp.sum(jnp.sum(total * total, axis=0, keepdims=True), axis=1, keepdims=True)
            row = jnp.where(lane == at, square, row)
            at += 1
    norms = jnp.sqrt(row)
    row_out[...] = norms
    peak_out[...] = jnp.broadcast_to(jnp.max(norms, axis=1, keepdims=True), peak_out.shape)


def block_norms(pairs):
    shape = jax.ShapeDtypeStruct((8, BLOCK), jnp.float32)
    args = [x for pair in pairs for x in pair]
    return call(norm_kernel, [shape, shape], args, [VMEM] * len(args), [VMEM] * 2)


def peak_rounds():
    rounds = [("blk", [1])]
    for axis, low in (("blk", 2), ("tok", 1)):
        size = lax.axis_size(axis)
        while low < size:
            rounds.append((axis, [m for m in (low, 2 * low, 3 * low) if m < size]))
            low *= 4
    return rounds


def max_kernel(*refs):
    total = refs[0][...]
    for other in refs[1:-1]:
        total = jnp.maximum(total, other[...])
    refs[-1][...] = total


def score_kernel(row, *refs):
    peak = refs[0][...]
    for other in refs[1:-1]:
        peak = jnp.maximum(peak, other[...])
    out = refs[-1]
    score = row[...] / (peak + 1e-06)
    out[...] = score[0:1, 0 : out.shape[1]]


def scores(row, peak, count):
    rounds = peak_rounds()
    for n, (axis, masks) in enumerate(rounds):
        got = [peak] + [swap(peak, axis, m) for m in masks]
        if n < len(rounds) - 1:
            peak = functools.reduce(jnp.maximum, got)
    return call(
        score_kernel,
        jax.ShapeDtypeStruct((1, count), jnp.float32),
        [row] + got,
        [VMEM] * (1 + len(got)),
        VMEM,
    )


def kept_kernel(keep, got, out):
    out[0] = (keep[...] + got[...]).astype(out.dtype)


def local(acts, out_grad, kept_ids, cand_ids):
    toks = lax.axis_size("tok")
    me = lax.axis_index("blk")
    pos = jnp.stack([me, lax.axis_index("tok")]).astype(jnp.int32)
    ncols = out_grad.shape[1] // BLOCK
    ks = kept_ids.shape[1]
    kept_share, cand_share = ks // toks, cand_ids.shape[1] // toks
    ids = jnp.concatenate([kept_ids, cand_ids], axis=1)
    cols = ids % ncols
    rows = lax.dynamic_index_in_dim(ids, me, 0, keepdims=False) // ncols
    width = acts.shape[1] // ROWS
    move = exchange if out_grad.shape[0] % ROWS == 0 else exchange_plain

    half = cand_share // 2
    pairs = []
    acts_from = None
    for lo, hi in ((0, half), (half, cand_share)):
        slots = [ks + u * cand_share + k for u in range(toks) for k in range(lo, hi)]
        got = move(out_grad, cols, pos, slots, acts if acts_from is None else None)
        acts_from = acts_from or got
        first = lambda unit, lo=lo: ks + unit * cand_share + lo
        keep, send = products(
            acts_from, got, width, rows, pos, toks, hi - lo, first, jnp.bfloat16
        )
        pairs.append(halve(keep, send, hi - lo))
    got = move(out_grad, cols, pos, list(range(ks)))
    keep, send = products(
        acts_from, got, width, rows, pos, toks, kept_share, lambda u: u * kept_share, jnp.float32
    )
    kept_pair = halve(keep, send, kept_share)

    row, peak = block_norms(pairs)
    cand_score = scores(row, peak, cand_share)
    kept_grad = call(
        kept_kernel,
        jax.ShapeDtypeStruct((1, kept_share, BLOCK, BLOCK), jnp.bfloat16),
        kept_pair,
        [VMEM] * 2,
        VMEM,
    )
    return (kept_grad, cand_score)


def solution(mesh):
    return jax.shard_map(
        local,
        mesh=mesh,
        in_specs=(P("tok", "blk"), P(("tok", "blk"), None), P(), P()),
        out_specs=(P("blk", "tok", None, None), P("blk", "tok")),
        check_vma=False,
    )
```

time: 320 us -> 118 us (0.37)
  blocking collectives: 115 us -> 0 us
  other arithmetic: 37.6 us -> 0.19 us
  local copies, waits for them, and re-layouts: 42.6 us -> 8.67 us
  waiting for transfers between devices: 98.5 us -> 64.8 us
  starting transfers between devices: 5.25 us -> 33.5 us
  between operations: 14.9 us -> 0.85 us
  Pallas kernels: 0 us -> 9.38 us
  matrix products: 5.71 us -> 0 us
    psum x1 -> x0, blocking collectives: 75.6 us -> none  [local(): kept_full, cand_full = lax.psum((kept_part, cand_part), 'tok')]
    psum x1 -> x0, waiting for transfers between devices: 75.1 us -> none  [local(): kept_full, cand_full = lax.psum((kept_part, cand_part), 'tok')]
    ppermute x0 -> x34, waiting for transfers between devices: none -> 64.8 us  [swap(): return lax.ppermute(x, axis, [(i, i ^ mask) for i in range(size)])]
    pmax x1 -> x0, blocking collectives: 39.4 us -> none  [local(): peak = lax.pmax(jnp.max(norms), ('tok', 'blk'))]
    ppermute x0 -> x34, starting transfers between devices: none -> 33.5 us  [swap(): return lax.ppermute(x, axis, [(i, i ^ mask) for i in range(size)])]
    gather x18 -> x0, local copies, waits for them, and re-layouts: 27.6 us -> none  [the longest x4 8.96 us: one_group(): left = jnp.take(acts3, rows_here, axis=1)]
    all_to_all x1 -> x0, waiting for transfers between devices: 23.4 us -> none  [local(): lax.all_to_all(outgoing, 'blk', split_axis=1, concat_axis=0, tiled=True)]
    scatter-add x1 -> x0, other arithmetic: 22.3 us -> none  [column_table(): jnp.unique(cols, size=width, fill_value=0)]
  transfers between devices with their start and end apart: 3 -> 34, of which waited for: 2 -> 17; matrix products, arithmetic and copies ran while one was open for 15% -> 0% of each run, Pallas kernels for 0% -> 7%
where the time goes in v2:
time: 118 us; the launch traced here: 117 us
  waiting for transfers between devices  64.8 us (55%)
  starting transfers between devices  33.5 us (28%)
  Pallas kernels  9.38 us (8%)
  local copies, waits for them, and re-layouts  8.67 us (7%)
    ppermute x34, waiting for transfers between devices, swap(): return lax.ppermute(x, axis, [(i, i ^ mask) for i in range(size)])  64.8 us
    ppermute x34, starting transfers between devices, swap(): return lax.ppermute(x, axis, [(i, i ^ mask) for i in range(size)])  33.5 us
    pallas_call x12, Pallas kernels, call(): pl.pallas_call(kernel, out_shape=outs, in_specs=specs, out_specs=out_spec...  9.38 us
    unnamed x38, local copies, waits for them, and re-layouts  8.67 us
  transfers between devices with their start and end apart: 34, of which 17 were waited for; matrix products, arithmetic and copies ran while one was open for 0% of the time, Pallas kernels for 7%

profile of v2, /device:TPU:0, one launch (start us, length us, event | category | flops | bytes accessed | tf_op | source)
XLA Modules:
  0.0 117.4 jit_solution(16501993932936286435)
XLA Ops:
  6.1 3.4 %collective-permute-start.11 = (bf16[32,16,128]{2,1,0:T(8,128)(2,1)S(1)}, bf16[32,16,128]{2,1,0:T(8,128)(2,1)S(1)}, u32[]{:S(2)}, u32[]{:S(2)}) collective-permute-start(bf16[32,16,128]{2,1,0:T(8,128)(2,1)S(1)} %get-tuple-element.40), channel_id=1, source_target_pairs={{0,6},{1,7},{2,4},{3,5},{4,2},{5,3},{6,0},{7,1},{8,14},{9,15},{10,... | collective-permute-start | bytes 393224 | tf_op jit(solution)/shard_map/ppermute | solution.py:22
  11.2 1.5 %collective-permute-start.10 = (bf16[112,16,128]{2,1,0:T(8,128)(2,1)S(1)}, bf16[112,16,128]{2,1,0:T(8,128)(2,1)S(1)}, u32[]{:S(2)}, u32[]{:S(2)}) collective-permute-start(bf16[112,16,128]{2,1,0:T(8,128)(2,1)S(1)} %get-tuple-element.39), channel_id=1, source_target_pairs={{0,6},{1,7},{2,4},{3,5},{4,2},{5,3},{6,0},{7,1},{8,14},{9,15},{10,... | collective-permute-start | bytes 1376264 | tf_op jit(solution)/shard_map/ppermute | solution.py:22
  13.5 1.9 %collective-permute-start.7 = (bf16[32,16,128]{2,1,0:T(8,128)(2,1)S(1)}, bf16[32,16,128]{2,1,0:T(8,128)(2,1)S(1)}, u32[]{:S(2)}, u32[]{:S(2)}) collective-permute-start(bf16[32,16,128]{2,1,0:T(8,128)(2,1)S(1)} %get-tuple-element.38), channel_id=1, source_target_pairs={{0,4},{1,5},{2,6},{3,7},{4,0},{5,1},{6,2},{7,3},{8,12},{9,13},{10,... | collective-permute-start | bytes 393224 | tf_op jit(solution)/shard_map/ppermute | solution.py:22
  17.2 1.5 %collective-permute-start.19 = (bf16[48,16,128]{2,1,0:T(8,128)(2,1)S(1)}, bf16[48,16,128]{2,1,0:T(8,128)(2,1)S(1)}, u32[]{:S(2)}, u32[]{:S(2)}) collective-permute-start(bf16[48,16,128]{2,1,0:T(8,128)(2,1)S(1)} %get-tuple-element.51), channel_id=1, source_target_pairs={{0,2},{1,3},{2,0},{3,1},{4,6},{5,7},{6,4},{7,5},{8,10},{9,11},{10,... | collective-permute-start | bytes 589832 | tf_op jit(solution)/shard_map/ppermute | solution.py:22
  18.7 10.6 %collective-permute-done.7.refs_9_ = bf16[32,16,128]{2,1,0:T(8,128)(2,1)S(1)} collective-permute-done((bf16[32,16,128]{2,1,0:T(8,128)(2,1)S(1)}, bf16[32,16,128]{2,1,0:T(8,128)(2,1)S(1)}, u32[]{:S(2)}, u32[]{:S(2)}) %collective-permute-start.7) | collective-permute-done | bytes 131104 | tf_op jit(solution)/shard_map/ppermute | solution.py:22
  29.3 1.7 %collective-permute-start.21 = (bf16[48,16,128]{2,1,0:T(8,128)(2,1)S(1)}, bf16[48,16,128]{2,1,0:T(8,128)(2,1)}, u32[]{:S(2)}, u32[]{:S(2)}) collective-permute-start(bf16[48,16,128]{2,1,0:T(8,128)(2,1)S(1)} %get-tuple-element.52), channel_id=1, source_target_pairs={{0,4},{1,5},{2,6},{3,7},{4,0},{5,1},{6,2},{7,3},{8,12},{9,13},{10,... | collective-permute-start | bytes 589832 | tf_op jit(solution)/shard_map/ppermute | solution.py:22
  31.0 9.7 %collective-permute-done.19.refs_5_ = bf16[48,16,128]{2,1,0:T(8,128)(2,1)S(1)} collective-permute-done((bf16[48,16,128]{2,1,0:T(8,128)(2,1)S(1)}, bf16[48,16,128]{2,1,0:T(8,128)(2,1)S(1)}, u32[]{:S(2)}, u32[]{:S(2)}) %collective-permute-start.19) | collective-permute-done | bytes 196640 | tf_op jit(solution)/shard_map/ppermute | solution.py:22
  40.7 1.4 %collective-permute-start.23 = (bf16[48,16,128]{2,1,0:T(8,128)(2,1)S(1)}, bf16[48,16,128]{2,1,0:T(8,128)(2,1)}, u32[]{:S(2)}, u32[]{:S(2)}) collective-permute-start(bf16[48,16,128]{2,1,0:T(8,128)(2,1)S(1)} %get-tuple-element.53), channel_id=1, source_target_pairs={{0,6},{1,7},{2,4},{3,5},{4,2},{5,3},{6,0},{7,1},{8,14},{9,15},{10,... | collective-permute-start | bytes 589832 | tf_op jit(solution)/shard_map/ppermute | solution.py:22
  43.1 5.2 %collective-permute-done.23.refs_13_ = bf16[48,16,128]{2,1,0:T(8,128)(2,1)} collective-permute-done((bf16[48,16,128]{2,1,0:T(8,128)(2,1)S(1)}, bf16[48,16,128]{2,1,0:T(8,128)(2,1)}, u32[]{:S(2)}, u32[]{:S(2)}) %collective-permute-start.23) | collective-permute-done | bytes 196640 | tf_op jit(solution)/shard_map/ppermute | solution.py:22
  56.7 2.2 %shard_map.67 = (f32[12,128,128]{2,1,0:T(8,128)S(1)}, bf16[12,128,128]{2,1,0:T(8,128)(2,1)S(1)}) custom-call(s32[2]{0:T(128)S(1)} %pad_add_fusion.1.pos, s32[64]{0:T(128)S(1)} %bitcast_select_fusion.rows, bf16[88,16,128]{2,1,0:T(8,128)(2,1)S(1)} %get-tuple-element.31.refs_0_, bf16[24,16,128]{2,1,0:T(8,128)(2,1)S(1)} %copy-done.13, ...), custom_call_target="tpu_custom_call" | custom-call | tf_op jit(solution)/shard_map/pallas_call | solution.py:26
  59.0 1.6 %collective-permute-start.25 = (bf16[12,128,128]{2,1,0:T(8,128)(2,1)S(1)}, bf16[12,128,128]{2,1,0:T(8,128)(2,1)S(1)}, u32[]{:S(2)}, u32[]{:S(2)}) collective-permute-start(bf16[12,128,128]{2,1,0:T(8,128)(2,1)S(1)} %get-tuple-element.55), channel_id=1, source_target_pairs={{0,8},{8,0},{16,24},{24,16},{1,9},{9,1},{17,25},{25,17},{2,10},{10... | collective-permute-start | bytes 1179656 | tf_op jit(solution)/shard_map/ppermute | solution.py:22
  63.8 1.6 %collective-permute-start.14 = (f32[8,128,128]{2,1,0:T(8,128)S(1)}, f32[8,128,128]{2,1,0:T(8,128)S(1)}, u32[]{:S(2)}, u32[]{:S(2)}) collective-permute-start(f32[8,128,128]{2,1,0:T(8,128)S(1)} %get-tuple-element.42), channel_id=1, source_target_pairs={{0,8},{8,0},{16,24},{24,16},{1,9},{9,1},{17,25},{25,17},{2,10},{10... | collective-permute-start | bytes 1572872 | tf_op jit(solution)/shard_map/ppermute | solution.py:22
  65.4 5.6 %collective-permute-done.25.got = bf16[12,128,128]{2,1,0:T(8,128)(2,1)S(1)} collective-permute-done((bf16[12,128,128]{2,1,0:T(8,128)(2,1)S(1)}, bf16[12,128,128]{2,1,0:T(8,128)(2,1)S(1)}, u32[]{:S(2)}, u32[]{:S(2)}) %collective-permute-start.25) | collective-permute-done | bytes 393248 | tf_op jit(solution)/shard_map/ppermute | solution.py:22
  71.1 2.7 %collective-permute-start.26 = (bf16[6,128,128]{2,1,0:T(8,128)(2,1)S(1)}, bf16[6,128,128]{2,1,0:T(8,128)(2,1)S(1)}, u32[]{:S(2)}, u32[]{:S(2)}) collective-permute-start(bf16[6,128,128]{2,1,0:T(8,128)(2,1)S(1)} %get-tuple-element.57), channel_id=1, source_target_pairs={{0,16},{8,24},{16,0},{24,8},{1,17},{9,25},{17,1},{25,9},{2,18},{10... | collective-permute-start | bytes 589832 | tf_op jit(solution)/shard_map/ppermute | solution.py:22
  73.7 9.9 %collective-permute-done.16.got = bf16[12,128,128]{2,1,0:T(8,128)(2,1)S(1)} collective-permute-done((bf16[12,128,128]{2,1,0:T(8,128)(2,1)S(1)}, bf16[12,128,128]{2,1,0:T(8,128)(2,1)S(1)}, u32[]{:S(2)}, u32[]{:S(2)}) %collective-permute-start.16) | collective-permute-done | bytes 393248 | tf_op jit(solution)/shard_map/ppermute | solution.py:22
  83.7 1.7 %collective-permute-start.17 = (bf16[6,128,128]{2,1,0:T(8,128)(2,1)S(1)}, bf16[6,128,128]{2,1,0:T(8,128)(2,1)S(1)}, u32[]{:S(2)}, u32[]{:S(2)}) collective-permute-start(bf16[6,128,128]{2,1,0:T(8,128)(2,1)S(1)} %get-tuple-element.48), channel_id=1, source_target_pairs={{0,16},{8,24},{16,0},{24,8},{1,17},{9,25},{17,1},{25,9},{2,18},{10... | collective-permute-start | bytes 589832 | tf_op jit(solution)/shard_map/ppermute | solution.py:22
  85.5 12.9 %collective-permute-done.14.got = f32[8,128,128]{2,1,0:T(8,128)S(1)} collective-permute-done((f32[8,128,128]{2,1,0:T(8,128)S(1)}, f32[8,128,128]{2,1,0:T(8,128)S(1)}, u32[]{:S(2)}, u32[]{:S(2)}) %collective-permute-start.14) | collective-permute-done | bytes 524320 | tf_op jit(solution)/shard_map/ppermute | solution.py:22
  101.2 1.5 %collective-permute-start.28 = (f32[8,128]{1,0:T(8,128)S(1)}, f32[8,128]{1,0:T(8,128)S(1)}, u32[]{:S(2)}, u32[]{:S(2)}) collective-permute-start(f32[8,128]{1,0:T(8,128)S(1)} %max.12), channel_id=1, source_target_pairs={{0,2},{1,3},{2,0},{3,1},{4,6},{5,7},{6,4},{7,5},{8,10},{9,11},{10,... | collective-permute-start | bytes 12296 | tf_op jit(solution)/shard_map/ppermute | solution.py:22
  103.1 1.6 %collective-permute-start.30 = (f32[8,128]{1,0:T(8,128)S(1)}, f32[8,128]{1,0:T(8,128)S(1)}, u32[]{:S(2)}, u32[]{:S(2)}) collective-permute-start(f32[8,128]{1,0:T(8,128)S(1)} %max.12), channel_id=1, source_target_pairs={{0,6},{1,7},{2,4},{3,5},{4,2},{5,3},{6,0},{7,1},{8,14},{9,15},{10,... | collective-permute-start | bytes 12296 | tf_op jit(solution)/shard_map/ppermute | solution.py:22
  104.8 1.5 %collective-permute-done.29 = f32[8,128]{1,0:T(8,128)S(1)} collective-permute-done((f32[8,128]{1,0:T(8,128)S(1)}, f32[8,128]{1,0:T(8,128)S(1)}, u32[]{:S(2)}, u32[]{:S(2)}) %collective-permute-start.29) | collective-permute-done | bytes 4128 | tf_op jit(solution)/shard_map/ppermute | solution.py:22
  107.6 2.5 %collective-permute-start.31 = (f32[8,128]{1,0:T(8,128)S(1)}, f32[8,128]{1,0:T(8,128)S(1)}, u32[]{:S(2)}, u32[]{:S(2)}) collective-permute-start(f32[8,128]{1,0:T(8,128)S(1)} %maximum_maximum_fusion.refs_0_), channel_id=1, source_target_pairs={{0,8},{8,0},{16,24},{24,16},{1,9},{9,1},{17,25},{25,17},{2,10},{10... | collective-permute-start | bytes 12296 | tf_op jit(solution)/shard_map/ppermute | solution.py:22
  110.8 1.7 %collective-permute-start.33 = (f32[8,128]{1,0:T(8,128)S(1)}, f32[8,128]{1,0:T(8,128)S(1)}, u32[]{:S(2)}, u32[]{:S(2)}) collective-permute-start(f32[8,128]{1,0:T(8,128)S(1)} %maximum_maximum_fusion.refs_0_), channel_id=1, source_target_pairs={{0,24},{8,16},{16,8},{24,0},{1,25},{9,17},{17,9},{25,1},{2,26},{10... | collective-permute-start | bytes 12296 | tf_op jit(solution)/shard_map/ppermute | solution.py:22
  112.5 2.1 %collective-permute-done.32.refs_2_ = f32[8,128]{1,0:T(8,128)S(1)} collective-permute-done((f32[8,128]{1,0:T(8,128)S(1)}, f32[8,128]{1,0:T(8,128)S(1)}, u32[]{:S(2)}, u32[]{:S(2)}) %collective-permute-start.32) | collective-permute-done | bytes 4128 | tf_op jit(solution)/shard_map/ppermute | solution.py:22
  114.6 1.6 %collective-permute-done.33.refs_3_ = f32[8,128]{1,0:T(8,128)S(1)} collective-permute-done((f32[8,128]{1,0:T(8,128)S(1)}, f32[8,128]{1,0:T(8,128)S(1)}, u32[]{:S(2)}, u32[]{:S(2)}) %collective-permute-start.33) | collective-permute-done | bytes 4128 | tf_op jit(solution)/shard_map/ppermute | solution.py:22
  (99 shorter events, 28.7 us)
Async XLA Ops:
  4.2 8.6 %collective-permute-start.18 = (bf16[24,16,128]{2,1,0:T(8,128)(2,1)S(1)}, bf16[24,16,128]{2,1,0:T(8,128)(2,1)S(1)}, u32[]{:S(2)}, u32[]{:S(2)}) collective-permute-start(bf16[24,16,128]{2,1,0:T(8,128)(2,1)S(1)} %get-tuple-element.50), channel_id=1, source_target_pairs={{0,1},{1,0},{2,3},{3,2},{4,5},{5,4},{6,7},{7,6},{8,9},{9,8},{10,11... | collective-permute-start | bytes 294920 | tf_op jit(solution)/shard_map/ppermute | solution.py:22
  6.1 9.3 %collective-permute-start.11 = (bf16[32,16,128]{2,1,0:T(8,128)(2,1)S(1)}, bf16[32,16,128]{2,1,0:T(8,128)(2,1)S(1)}, u32[]{:S(2)}, u32[]{:S(2)}) collective-permute-start(bf16[32,16,128]{2,1,0:T(8,128)(2,1)S(1)} %get-tuple-element.40), channel_id=1, source_target_pairs={{0,6},{1,7},{2,4},{3,5},{4,2},{5,3},{6,0},{7,1},{8,14},{9,15},{10,... | collective-permute-start | bytes 393224 | tf_op jit(solution)/shard_map/ppermute | solution.py:22
  9.6 7.6 %collective-permute-start.3 = (bf16[32,16,128]{2,1,0:T(8,128)(2,1)S(1)}, bf16[32,16,128]{2,1,0:T(8,128)(2,1)S(1)}, u32[]{:S(2)}, u32[]{:S(2)}) collective-permute-start(bf16[32,16,128]{2,1,0:T(8,128)(2,1)S(1)} %get-tuple-element.36), channel_id=1, source_target_pairs={{0,2},{1,3},{2,0},{3,1},{4,6},{5,7},{6,4},{7,5},{8,10},{9,11},{10,... | collective-permute-start | bytes 393224 | tf_op jit(solution)/shard_map/ppermute | solution.py:22
  11.2 31.3 %collective-permute-start.10 = (bf16[112,16,128]{2,1,0:T(8,128)(2,1)S(1)}, bf16[112,16,128]{2,1,0:T(8,128)(2,1)S(1)}, u32[]{:S(2)}, u32[]{:S(2)}) collective-permute-start(bf16[112,16,128]{2,1,0:T(8,128)(2,1)S(1)} %get-tuple-element.39), channel_id=1, source_target_pairs={{0,6},{1,7},{2,4},{3,5},{4,2},{5,3},{6,0},{7,1},{8,14},{9,15},{10,... | collective-permute-start | bytes 1376264 | tf_op jit(solution)/shard_map/ppermute | solution.py:22
  12.7 30.3 %collective-permute-start.2 = (bf16[112,16,128]{2,1,0:T(8,128)(2,1)S(1)}, bf16[112,16,128]{2,1,0:T(8,128)(2,1)S(1)}, u32[]{:S(2)}, u32[]{:S(2)}) collective-permute-start(bf16[112,16,128]{2,1,0:T(8,128)(2,1)S(1)} %get-tuple-element.35), channel_id=1, source_target_pairs={{0,2},{1,3},{2,0},{3,1},{4,6},{5,7},{6,4},{7,5},{8,10},{9,11},{10,... | collective-permute-start | bytes 1376264 | tf_op jit(solution)/shard_map/ppermute | solution.py:22
  13.5 15.8 %collective-permute-start.7 = (bf16[32,16,128]{2,1,0:T(8,128)(2,1)S(1)}, bf16[32,16,128]{2,1,0:T(8,128)(2,1)S(1)}, u32[]{:S(2)}, u32[]{:S(2)}) collective-permute-start(bf16[32,16,128]{2,1,0:T(8,128)(2,1)S(1)} %get-tuple-element.38), channel_id=1, source_target_pairs={{0,4},{1,5},{2,6},{3,7},{4,0},{5,1},{6,2},{7,3},{8,12},{9,13},{10,... | collective-permute-start | bytes 393224 | tf_op jit(solution)/shard_map/ppermute | solution.py:22
  15.4 33.6 %collective-permute-start.6 = (bf16[112,16,128]{2,1,0:T(8,128)(2,1)S(1)}, bf16[112,16,128]{2,1,0:T(8,128)(2,1)S(1)}, u32[]{:S(2)}, u32[]{:S(2)}) collective-permute-start(bf16[112,16,128]{2,1,0:T(8,128)(2,1)S(1)} %get-tuple-element.37), channel_id=1, source_target_pairs={{0,4},{1,5},{2,6},{3,7},{4,0},{5,1},{6,2},{7,3},{8,12},{9,13},{10,... | collective-permute-start | bytes 1376264 | tf_op jit(solution)/shard_map/ppermute | solution.py:22
  17.2 23.5 %collective-permute-start.19 = (bf16[48,16,128]{2,1,0:T(8,128)(2,1)S(1)}, bf16[48,16,128]{2,1,0:T(8,128)(2,1)S(1)}, u32[]{:S(2)}, u32[]{:S(2)}) collective-permute-start(bf16[48,16,128]{2,1,0:T(8,128)(2,1)S(1)} %get-tuple-element.51), channel_id=1, source_target_pairs={{0,2},{1,3},{2,0},{3,1},{4,6},{5,7},{6,4},{7,5},{8,10},{9,11},{10,... | collective-permute-start | bytes 589832 | tf_op jit(solution)/shard_map/ppermute | solution.py:22
  29.3 13.2 %collective-permute-start.21 = (bf16[48,16,128]{2,1,0:T(8,128)(2,1)S(1)}, bf16[48,16,128]{2,1,0:T(8,128)(2,1)}, u32[]{:S(2)}, u32[]{:S(2)}) collective-permute-start(bf16[48,16,128]{2,1,0:T(8,128)(2,1)S(1)} %get-tuple-element.52), channel_id=1, source_target_pairs={{0,4},{1,5},{2,6},{3,7},{4,0},{5,1},{6,2},{7,3},{8,12},{9,13},{10,... | collective-permute-start | bytes 589832 | tf_op jit(solution)/shard_map/ppermute | solution.py:22
  40.7 7.6 %collective-permute-start.23 = (bf16[48,16,128]{2,1,0:T(8,128)(2,1)S(1)}, bf16[48,16,128]{2,1,0:T(8,128)(2,1)}, u32[]{:S(2)}, u32[]{:S(2)}) collective-permute-start(bf16[48,16,128]{2,1,0:T(8,128)(2,1)S(1)} %get-tuple-element.53), channel_id=1, source_target_pairs={{0,6},{1,7},{2,4},{3,5},{4,2},{5,3},{6,0},{7,1},{8,14},{9,15},{10,... | collective-permute-start | bytes 589832 | tf_op jit(solution)/shard_map/ppermute | solution.py:22
  42.5 7.0 %collective-permute-start = (bf16[88,16,128]{2,1,0:T(8,128)(2,1)S(1)}, bf16[88,16,128]{2,1,0:T(8,128)(2,1)S(1)}, u32[]{:S(2)}, u32[]{:S(2)}) collective-permute-start(bf16[88,16,128]{2,1,0:T(8,128)(2,1)S(1)} %get-tuple-element.33), channel_id=1, source_target_pairs={{0,1},{1,0},{2,3},{3,2},{4,5},{5,4},{6,7},{7,6},{8,9},{9,8},{10,11... | collective-permute-start | bytes 1081352 | tf_op jit(solution)/shard_map/ppermute | solution.py:22
  42.5 10.0 %collective-permute-start.12 = (bf16[112,16,128]{2,1,0:T(8,128)(2,1)S(1)}, bf16[112,16,128]{2,1,0:T(8,128)(2,1)S(1)}, u32[]{:S(2)}, u32[]{:S(2)}) collective-permute-start(bf16[112,16,128]{2,1,0:T(8,128)(2,1)S(1)} %collective-permute-done.10.refs_12_.refs_6_), channel_id=1, source_target_pairs={{0,1},{1,0},{2,3},{3,2},{4,5},{5,4},{6,7},{7,6},{8,9},{9,8},{10,11... | collective-permute-start | bytes 1376264 | tf_op jit(solution)/shard_map/ppermute | solution.py:22
  43.0 9.7 %collective-permute-start.4 = (bf16[112,16,128]{2,1,0:T(8,128)(2,1)S(1)}, bf16[112,16,128]{2,1,0:T(8,128)(2,1)S(1)}, u32[]{:S(2)}, u32[]{:S(2)}) collective-permute-start(bf16[112,16,128]{2,1,0:T(8,128)(2,1)S(1)} %collective-permute-done.2.refs_4_.refs_2_), channel_id=1, source_target_pairs={{0,1},{1,0},{2,3},{3,2},{4,5},{5,4},{6,7},{7,6},{8,9},{9,8},{10,11... | collective-permute-start | bytes 1376264 | tf_op jit(solution)/shard_map/ppermute | solution.py:22
  51.6 10.4 %collective-permute-start.1 = (bf16[16,16,128]{2,1,0:T(8,128)(2,1)}, bf16[16,16,128]{2,1,0:T(8,128)(2,1)S(1)}, u32[]{:S(2)}, u32[]{:S(2)}) collective-permute-start(bf16[16,16,128]{2,1,0:T(8,128)(2,1)} %copy-done.16), channel_id=1, source_target_pairs={{0,1},{1,0},{2,3},{3,2},{4,5},{5,4},{6,7},{7,6},{8,9},{9,8},{10,11... | collective-permute-start | bytes 196616 | tf_op jit(solution)/shard_map/ppermute | solution.py:22
  52.3 10.2 %collective-permute-start.13 = (bf16[32,16,128]{2,1,0:T(8,128)(2,1)}, bf16[32,16,128]{2,1,0:T(8,128)(2,1)S(1)}, u32[]{:S(2)}, u32[]{:S(2)}) collective-permute-start(bf16[32,16,128]{2,1,0:T(8,128)(2,1)} %copy-done.6), channel_id=1, source_target_pairs={{0,1},{1,0},{2,3},{3,2},{4,5},{5,4},{6,7},{7,6},{8,9},{9,8},{10,11... | collective-permute-start | bytes 393224 | tf_op jit(solution)/shard_map/ppermute | solution.py:22
  52.5 10.0 %collective-permute-start.5 = (bf16[32,16,128]{2,1,0:T(8,128)(2,1)}, bf16[32,16,128]{2,1,0:T(8,128)(2,1)S(1)}, u32[]{:S(2)}, u32[]{:S(2)}) collective-permute-start(bf16[32,16,128]{2,1,0:T(8,128)(2,1)} %copy-done.8), channel_id=1, source_target_pairs={{0,1},{1,0},{2,3},{3,2},{4,5},{5,4},{6,7},{7,6},{8,9},{9,8},{10,11... | collective-permute-start | bytes 393224 | tf_op jit(solution)/shard_map/ppermute | solution.py:22
  52.8 9.7 %collective-permute-start.9 = (bf16[32,16,128]{2,1,0:T(8,128)(2,1)}, bf16[32,16,128]{2,1,0:T(8,128)(2,1)S(1)}, u32[]{:S(2)}, u32[]{:S(2)}) collective-permute-start(bf16[32,16,128]{2,1,0:T(8,128)(2,1)} %copy-done.10), channel_id=1, source_target_pairs={{0,1},{1,0},{2,3},{3,2},{4,5},{5,4},{6,7},{7,6},{8,9},{9,8},{10,11... | collective-permute-start | bytes 393224 | tf_op jit(solution)/shard_map/ppermute | solution.py:22
  59.0 12.0 %collective-permute-start.25 = (bf16[12,128,128]{2,1,0:T(8,128)(2,1)S(1)}, bf16[12,128,128]{2,1,0:T(8,128)(2,1)S(1)}, u32[]{:S(2)}, u32[]{:S(2)}) collective-permute-start(bf16[12,128,128]{2,1,0:T(8,128)(2,1)S(1)} %get-tuple-element.55), channel_id=1, source_target_pairs={{0,8},{8,0},{16,24},{24,16},{1,9},{9,1},{17,25},{25,17},{2,10},{10... | collective-permute-start | bytes 1179656 | tf_op jit(solution)/shard_map/ppermute | solution.py:22
  62.0 21.7 %collective-permute-start.16 = (bf16[12,128,128]{2,1,0:T(8,128)(2,1)S(1)}, bf16[12,128,128]{2,1,0:T(8,128)(2,1)S(1)}, u32[]{:S(2)}, u32[]{:S(2)}) collective-permute-start(bf16[12,128,128]{2,1,0:T(8,128)(2,1)S(1)} %get-tuple-element.46), channel_id=1, source_target_pairs={{0,8},{8,0},{16,24},{24,16},{1,9},{9,1},{17,25},{25,17},{2,10},{10... | collective-permute-start | bytes 1179656 | tf_op jit(solution)/shard_map/ppermute | solution.py:22
  63.8 34.6 %collective-permute-start.14 = (f32[8,128,128]{2,1,0:T(8,128)S(1)}, f32[8,128,128]{2,1,0:T(8,128)S(1)}, u32[]{:S(2)}, u32[]{:S(2)}) collective-permute-start(f32[8,128,128]{2,1,0:T(8,128)S(1)} %get-tuple-element.42), channel_id=1, source_target_pairs={{0,8},{8,0},{16,24},{24,16},{1,9},{9,1},{17,25},{25,17},{2,10},{10... | collective-permute-start | bytes 1572872 | tf_op jit(solution)/shard_map/ppermute | solution.py:22
  71.1 28.6 %collective-permute-start.26 = (bf16[6,128,128]{2,1,0:T(8,128)(2,1)S(1)}, bf16[6,128,128]{2,1,0:T(8,128)(2,1)S(1)}, u32[]{:S(2)}, u32[]{:S(2)}) collective-permute-start(bf16[6,128,128]{2,1,0:T(8,128)(2,1)S(1)} %get-tuple-element.57), channel_id=1, source_target_pairs={{0,16},{8,24},{16,0},{24,8},{1,17},{9,25},{17,1},{25,9},{2,18},{10... | collective-permute-start | bytes 589832 | tf_op jit(solution)/shard_map/ppermute | solution.py:22
  83.7 16.0 %collective-permute-start.17 = (bf16[6,128,128]{2,1,0:T(8,128)(2,1)S(1)}, bf16[6,128,128]{2,1,0:T(8,128)(2,1)S(1)}, u32[]{:S(2)}, u32[]{:S(2)}) collective-permute-start(bf16[6,128,128]{2,1,0:T(8,128)(2,1)S(1)} %get-tuple-element.48), channel_id=1, source_target_pairs={{0,16},{8,24},{16,0},{24,8},{1,17},{9,25},{17,1},{25,9},{2,18},{10... | collective-permute-start | bytes 589832 | tf_op jit(solution)/shard_map/ppermute | solution.py:22
  98.5 18.3 %collective-permute-start.15 = (f32[4,128,128]{2,1,0:T(8,128)S(1)}, f32[4,128,128]{2,1,0:T(8,128)S(1)}, u32[]{:S(2)}, u32[]{:S(2)}) collective-permute-start(f32[4,128,128]{2,1,0:T(8,128)S(1)} %get-tuple-element.44), channel_id=1, source_target_pairs={{0,16},{8,24},{16,0},{24,8},{1,17},{9,25},{17,1},{25,9},{2,18},{10... | collective-permute-start | bytes 786440 | tf_op jit(solution)/shard_map/ppermute | solution.py:22
  110.8 5.4 %collective-permute-start.33 = (f32[8,128]{1,0:T(8,128)S(1)}, f32[8,128]{1,0:T(8,128)S(1)}, u32[]{:S(2)}, u32[]{:S(2)}) collective-permute-start(f32[8,128]{1,0:T(8,128)S(1)} %maximum_maximum_fusion.refs_0_), channel_id=1, source_target_pairs={{0,24},{8,16},{16,8},{24,0},{1,25},{9,17},{17,9},{25,1},{2,26},{10... | collective-permute-start | bytes 12296 | tf_op jit(solution)/shard_map/ppermute | solution.py:22
  (29 other events, 138.4 us)

commit v3 on v2

v3 whole, which is shorter than its diff:
```python
import functools

import jax
import jax.numpy as jnp
from jax import lax
from jax.experimental import pallas as pl
from jax.experimental.pallas import tpu as pltpu
from jax.sharding import PartitionSpec as P

BLOCK = 128
ROWS = 16
FIRST = 6
PER_BLOCK = BLOCK // ROWS
VMEM_LIMIT = 16 * 1024 * 1024
ANY = pl.BlockSpec(memory_space=pl.ANY)
VMEM = pl.BlockSpec(memory_space=pltpu.VMEM)
SMEM = pl.BlockSpec(memory_space=pltpu.SMEM)
COST = pl.CostEstimate(flops=1, bytes_accessed=1, transcendentals=0)
PARAMS = pltpu.CompilerParams(vmem_limit_bytes=VMEM_LIMIT)


def swap(x, axis, mask):
    size = lax.axis_size(axis)
    return lax.ppermute(x, axis, [(i, i ^ mask) for i in range(size)])


def after(x, *others):
    return lax.optimization_barrier((x, others))[0]


def call(kernel, outs, args, specs, out_specs, scratch=()):
    return pl.pallas_call(
        kernel,
        out_shape=outs,
        in_specs=specs,
        out_specs=out_specs,
        scratch_shapes=scratch,
        compiler_params=PARAMS,
        cost_estimate=COST,
    )(*args)


def pack_kernel(slots, masks, acts_width, extra, pos, cols, grad, *refs):
    me = pos[0]
    acts = refs[:1] if acts_width else ()
    others = refs[len(acts) : len(refs) - len(masks)]
    outs = refs[len(refs) - len(masks) :]
    for acts_ref in acts:
        for row in range(acts_width // BLOCK):
            block = acts_ref[:, row * BLOCK : (row + 1) * BLOCK].T
            block = block.reshape(PER_BLOCK, ROWS, BLOCK)
            for out in outs:
                out[row * PER_BLOCK : (row + 1) * PER_BLOCK] = block
    for out, dests in zip(outs, masks):
        at = acts_width // ROWS
        for mask in dests:
            dest = me ^ mask
            for slot in slots:
                start = pl.multiple_of(cols[dest, slot] * BLOCK, BLOCK)
                out[at] = grad[:, pl.ds(start, BLOCK)]
                at += 1
            for other in others:
                out[at : at + extra] = other[pl.ds(dest * extra, extra)]
                at += extra


def owner_masks():
    return [(0,), (1,)] + [(m, m + 1) for m in range(2, lax.axis_size("blk"), 2)]


def pack(out_grad, cols, pos, slots, acts=None, others=()):
    masks = owner_masks()
    width = 0 if acts is None else acts.shape[1]
    extra = others[0].shape[0] // lax.axis_size("blk") if others else 0
    count = len(slots) + extra * len(others)
    more = list(others) if acts is None else [acts]
    return call(
        functools.partial(pack_kernel, slots, masks, width, extra),
        [
            jax.ShapeDtypeStruct((width // ROWS + len(d) * count, ROWS, BLOCK), out_grad.dtype)
            for d in masks
        ],
        [pos, cols, out_grad] + more,
        [SMEM, SMEM] + [VMEM] * (1 + len(more)),
        [VMEM] * len(masks),
    )


def exchange(buffers):
    owners = lax.axis_size("blk")
    got = [None] * owners
    got[0] = buffers[0]
    for mask in range(owners - 2, 1, -2):
        got[mask] = swap(buffers[mask // 2 + 1], "blk", mask)
    got[1] = swap(buffers[1], "blk", 1)
    return got


def forward(got, count, *others):
    owners = len(got)
    base = got[0].shape[0] - count
    even = range(2, owners, 2)
    chips = after([got[m] for m in even], got[1], *others)
    for mask, buffer in zip(even, chips):
        got[mask] = buffer
        got[mask + 1] = swap(buffer, "blk", 1)
    return [(buffer, base + (count if m % 2 and m > 1 else 0)) for m, buffer in enumerate(got)]


def columns_plain(out_grad, cols, slots):
    owners = lax.axis_size("blk")
    rows = out_grad.shape[0]
    count = len(slots)
    grad3 = out_grad.reshape(rows, -1, BLOCK)
    outgoing = jnp.take(grad3, cols[:, jnp.array(slots)].reshape(-1), axis=1)
    outgoing = outgoing.reshape(rows, owners, count, BLOCK).transpose(1, 2, 0, 3)
    incoming = lax.all_to_all(outgoing, "blk", 0, 0, tiled=True)
    return jnp.swapaxes(incoming, 0, 1).reshape(count * PER_BLOCK, ROWS, BLOCK)


def kept_units(units, mask):
    return [unit for unit in units if not unit & mask]


def product_kernel(plan, toks, bounds, first, spare, pos, rows, *refs):
    copies_of, inputs = plan
    srcs = refs[:inputs]
    *outs, acts_all, grad_all, sem = refs[inputs:]
    keeps, sends = outs[: len(bounds)], outs[len(bounds) : 2 * len(bounds)]
    spares = outs[2 * len(bounds) :]
    share = bounds[-1][1]
    me, tok = pos[0], pos[1]
    copies = []
    for n, (which, src, begin, size, peer) in enumerate(copies_of):
        at = 0 if peer is None else me ^ peer
        from_ref = srcs[src].at[pl.ds(begin, size)]
        if which == "acts":
            dst = acts_all.at[pl.ds(pl.multiple_of(at * size, size), size)]
        elif peer is None:
            dst = grad_all
            from_ref = from_ref.reshape(grad_all.shape)
        else:
            dst = grad_all.at[:, pl.ds(pl.multiple_of(at * ROWS, ROWS), ROWS)]
        copies.append(pltpu.make_async_copy(from_ref, dst, sem.at[n]))
    for copy in copies:
        copy.start()
    for copy in copies:
        copy.wait()
    for peer in range(toks if spares else 0):
        for k in range(spare):
            row = rows[me, (tok ^ peer) * spare + k] * PER_BLOCK
            block = acts_all[pl.ds(pl.multiple_of(row, PER_BLOCK), PER_BLOCK)]
            spares[peer % 2][peer // 2 * spare + k] = block.reshape(BLOCK, BLOCK)
    for peer in range(toks):
        unit = tok ^ peer
        for k in range(share):
            slot = unit * share + k
            row = rows[me, first + slot] * PER_BLOCK
            left = acts_all[pl.ds(pl.multiple_of(row, PER_BLOCK), PER_BLOCK)]
            prod = jnp.dot(
                left.reshape(BLOCK, BLOCK), grad_all[slot], preferred_element_type=jnp.float32
            )
            for (lo, hi, mask), keep, send in zip(bounds, keeps, sends):
                if lo <= k < hi:
                    out = send if peer & mask else keep
                    at = kept_units(range(toks), mask).index(peer & ~mask)
                    out[at * (hi - lo) + k - lo] = prod.astype(out.dtype)


def gather_plan(owners, width, count, acts_from, grads_from):
    buffers = []
    copies = []

    def index(buffer):
        for n, other in enumerate(buffers):
            if other is buffer:
                return n
        buffers.append(buffer)
        return len(buffers) - 1

    if isinstance(acts_from, list):
        for peer in range(owners):
            copies.append(("acts", index(acts_from[peer][0]), 0, width, peer))
    elif acts_from is not None:
        copies.append(("acts", index(acts_from), 0, acts_from.shape[0], None))
    if isinstance(grads_from, list):
        for peer in range(owners):
            buffer, begin = grads_from[peer]
            copies.append(("grad", index(buffer), begin, count, peer))
    else:
        copies.append(("grad", index(grads_from), 0, grads_from.shape[0], None))
    return buffers, copies


def products(acts_from, grads_from, width, rows, pos, bounds, first, dtype, spare=0):
    owners, toks = lax.axis_size("blk"), lax.axis_size("tok")
    count = toks * bounds[-1][1]
    buffers, copies = gather_plan(owners, width, count, acts_from, grads_from)
    sizes = [toks // 2 * (hi - lo) for lo, hi, _ in bounds]
    spares = 2 if spare else 0
    return call(
        functools.partial(
            product_kernel, (copies, len(buffers)), toks, bounds, first, spare
        ),
        [jax.ShapeDtypeStruct((n, BLOCK, BLOCK), jnp.float32) for n in sizes]
        + [jax.ShapeDtypeStruct((n, BLOCK, BLOCK), dtype) for n in sizes]
        + [jax.ShapeDtypeStruct((toks // 2 * spare, BLOCK, BLOCK), jnp.bfloat16)] * spares,
        [pos, rows] + buffers,
        [SMEM, SMEM] + [ANY] * len(buffers),
        [VMEM] * (2 * len(bounds) + spares),
        [
            pltpu.VMEM((owners * width, ROWS, BLOCK), jnp.bfloat16),
            pltpu.VMEM((count, BLOCK, BLOCK), jnp.bfloat16),
            pltpu.SemaphoreType.DMA((len(copies),)),
        ],
    )


def kept_pack_kernel(share, pos, cols, grad, *outs):
    units = 2 * outs[0].shape[0] // share // cols.shape[0]
    for peer in range(units):
        unit = pos[1] ^ peer
        out = outs[peer % 2]
        for dest in range(cols.shape[0]):
            for k in range(share):
                start = pl.multiple_of(cols[dest, unit * share + k] * BLOCK, BLOCK)
                at = (dest * (units // 2) + peer // 2) * share + k
                out[at] = grad[:, pl.ds(start, BLOCK)]


def kept_pack(out_grad, cols, pos, share):
    owners, toks = lax.axis_size("blk"), lax.axis_size("tok")
    shape = (owners * (toks // 2) * share, ROWS, BLOCK)
    return call(
        functools.partial(kept_pack_kernel, share),
        [jax.ShapeDtypeStruct(shape, out_grad.dtype)] * 2,
        (pos, cols, out_grad),
        [SMEM, SMEM, VMEM],
        [VMEM] * 2,
    )


def kept_product_kernel(copies_of, inputs, share, pos, *refs):
    srcs = refs[:inputs]
    lefts = refs[inputs : inputs + 2]
    keep, send, grad_all, sem = refs[inputs + 2 :]
    copies = []
    for n, (_, src, begin, size, peer) in enumerate(copies_of):
        at = pl.multiple_of((pos[0] ^ peer) * ROWS, ROWS)
        copies.append(
            pltpu.make_async_copy(
                srcs[src].at[pl.ds(begin, size)], grad_all.at[:, pl.ds(at, ROWS)], sem.at[n]
            )
        )
    for copy in copies:
        copy.start()
    for copy in copies:
        copy.wait()
    half = lefts[0].shape[0]
    for k in range(half):
        total = jnp.zeros((BLOCK, BLOCK), jnp.float32)
        for part, left in enumerate(lefts):
            total += jnp.dot(
                left[k], grad_all[part * half + k], preferred_element_type=jnp.float32
            )
        unit, slot = divmod(k, share)
        (send if unit % 2 else keep)[unit // 2 * share + slot] = total


def kept_product(lefts, grads_from, pos, share):
    owners = lax.axis_size("blk")
    half = lefts[0].shape[0]
    buffers, copies = gather_plan(owners, 0, 2 * half, None, grads_from)
    return call(
        functools.partial(kept_product_kernel, copies, len(buffers), share),
        [jax.ShapeDtypeStruct((half // 2, BLOCK, BLOCK), jnp.float32)] * 2,
        [pos] + buffers + lefts,
        [SMEM] + [ANY] * len(buffers) + [VMEM] * 2,
        [VMEM] * 2,
        [
            pltpu.VMEM((2 * half, BLOCK, BLOCK), jnp.bfloat16),
            pltpu.SemaphoreType.DMA((len(copies),)),
        ],
    )


def add_kernel(share, units, mask, keep, got, keep_out, send_out):
    for at, unit in enumerate(kept_units(units, mask)):
        for out, source in ((keep_out, unit), (send_out, unit | mask)):
            begin = units.index(source) * share
            for k in range(share):
                total = keep[begin + k] + got[begin + k].astype(jnp.float32)
                out[at * share + k] = total.astype(out.dtype)


def add(keep, got, share, dtype, units, mask):
    half = keep.shape[0] // 2
    return call(
        functools.partial(add_kernel, share, units, mask),
        [
            jax.ShapeDtypeStruct((half, BLOCK, BLOCK), jnp.float32),
            jax.ShapeDtypeStruct((half, BLOCK, BLOCK), dtype),
        ],
        (keep, got),
        [VMEM] * 2,
        [VMEM] * 2,
    )


def halve(keep, send, share, masks, units=None):
    units = kept_units(units or range(lax.axis_size("tok")), masks[0])
    got = swap(send, "tok", masks[0])
    for mask in masks[1:]:
        keep, send = add(keep, got, share, send.dtype, units, mask)
        units = kept_units(units, mask)
        got = swap(send, "tok", mask)
    return keep, got


def norm_kernel(*refs):
    row_out, peak_out = refs[-2:]
    lane = lax.broadcasted_iota(jnp.int32, row_out.shape, 1)
    row = jnp.zeros(row_out.shape, jnp.float32)
    at = 0
    for keep, got in zip(refs[:-2:2], refs[1:-2:2]):
        for k in range(keep.shape[0]):
            total = keep[k] + got[k].astype(jnp.float32)
            square = jnp.sum(jnp.sum(total * total, axis=0, keepdims=True), axis=1, keepdims=True)
            row = jnp.where(lane == at, square, row)
            at += 1
    row = jnp.sqrt(row)
    row_out[...] = row
    peak_out[...] = jnp.broadcast_to(jnp.max(row[0:1], axis=1, keepdims=True), peak_out.shape)


def block_norms(*pairs):
    devices = lax.axis_size("tok") * lax.axis_size("blk")
    args = [x for pair in pairs for x in pair]
    return call(
        norm_kernel,
        [jax.ShapeDtypeStruct((n, BLOCK), jnp.float32) for n in (8, devices)],
        args,
        [VMEM] * len(args),
        [VMEM] * 2,
    )


def result_kernel(row, peaks, keep, got, kept, score):
    peak = jnp.max(peaks[...], axis=0, keepdims=True)
    score[...] = (row[0:1, :] / (peak + 1e-06))[:, 0 : score.shape[1]]
    kept[0] = (keep[...] + got[...]).astype(kept.dtype)


def results(row, peak, count, pair):
    peaks = lax.all_to_all(peak, ("tok", "blk"), 0, 0, tiled=True)
    return call(
        result_kernel,
        [
            jax.ShapeDtypeStruct((1,) + pair[0].shape, jnp.bfloat16),
            jax.ShapeDtypeStruct((1, count), jnp.float32),
        ],
        (row, peaks) + pair,
        [VMEM] * 4,
        [VMEM] * 2,
    )


def local(acts, out_grad, kept_ids, cand_ids):
    toks = lax.axis_size("tok")
    me = lax.axis_index("blk")
    pos = jnp.stack([me, lax.axis_index("tok")]).astype(jnp.int32)
    ncols = out_grad.shape[1] // BLOCK
    ks = kept_ids.shape[1]
    kept_share, cand_share = ks // toks, cand_ids.shape[1] // toks
    ids = jnp.concatenate([kept_ids, cand_ids], axis=1)
    cols = ids % ncols
    rows = ids // ncols
    width = acts.shape[1] // ROWS

    half = FIRST * cand_share // 12
    up = [1 << n for n in range(toks.bit_length() - 1)]
    orders = (up, up[::-1])
    bounds = ((0, half, orders[0][0]), (half, cand_share, orders[1][0]))
    cands = list(range(ks, ks + toks * cand_share))
    bf16, f32 = jnp.bfloat16, jnp.float32
    if out_grad.shape[0] % ROWS:
        whole = lax.all_gather(acts.T, "blk", axis=0, tiled=True).reshape(-1, ROWS, BLOCK)
        keep0, keep1, send0, send1 = products(
            whole, columns_plain(out_grad, cols, cands), width, rows, pos, bounds, ks, bf16
        )
        keep2, send2 = products(
            whole,
            columns_plain(out_grad, cols, list(range(ks))),
            width,
            rows,
            pos,
            ((0, kept_share, 1),),
            0,
            f32,
        )
        row, peak = block_norms(
            halve(keep0, send0, half, orders[0]), halve(keep1, send1, cand_share - half, orders[1])
        )
        pair2 = halve(keep2, send2, kept_share, up)
    else:
        buffers0 = pack(out_grad, cols, pos, cands, acts)
        cols = after(cols, buffers0[0])
        kept = kept_pack(out_grad, cols, pos, kept_share)
        arrived0 = exchange(buffers0)
        kept = [kept[0], swap(kept[1], "tok", 1)]
        buffers2 = pack(out_grad, cols, pos, [], None, kept)
        from0 = forward(arrived0, len(cands), buffers2[0])
        keep0, keep1, send0, send1, left, left_sent = products(
            from0, from0, width, rows, pos, bounds, ks, bf16, kept_share
        )
        arrived2 = exchange(after(buffers2, keep1))
        from2 = forward(arrived2, ks)
        lefts = [left, swap(left_sent, "tok", 1)]
        row, peak = block_norms(
            halve(keep0, send0, half, orders[0]),
            halve(after(keep1, *arrived2[2::2]), send1, cand_share - half, orders[1]),
        )
        keep2, send2 = kept_product(lefts, from2, pos, kept_share)
        pair2 = halve(keep2, after(send2, row), kept_share, up[1:], range(0, toks, 2))

    kept_grad, cand_score = results(row, peak, cand_share, pair2)
    return (kept_grad, cand_score)


def solution(mesh):
    return jax.shard_map(
        local,
        mesh=mesh,
        in_specs=(P("tok", "blk"), P(("tok", "blk"), None), P(), P()),
        out_specs=(P("blk", "tok", None, None), P("blk", "tok")),
        check_vma=False,
    )
```

time: 118 us -> 94.1 us (0.80)
  waiting for transfers between devices: 64.8 us -> 48.9 us
  blocking collectives: 0 us -> 12.6 us
  starting transfers between devices: 33.5 us -> 21.8 us
  local copies, waits for them, and re-layouts: 8.67 us -> 2.74 us
  Pallas kernels: 9.38 us -> 6.85 us
    ppermute x34 -> x21, waiting for transfers between devices: 64.8 us -> 48.9 us  [swap(): return lax.ppermute(x, axis, [(i, i ^ mask) for i in range(size)])]
    all_to_all x0 -> x1, blocking collectives: none -> 12.6 us  [results(): peaks = lax.all_to_all(peak, ('tok', 'blk'), 0, 0, tiled=True)]
    ppermute x34 -> x21, starting transfers between devices: 33.5 us -> 21.8 us  [swap(): return lax.ppermute(x, axis, [(i, i ^ mask) for i in range(size)])]
    unnamed x38 -> x8, local copies, waits for them, and re-layouts: 8.67 us -> 2.74 us
    pallas_call x12 -> x9, Pallas kernels: 9.38 us -> 6.85 us  [call(): pl.pallas_call(kernel, out_shape=outs, in_specs=specs, out_specs=out_spec...]
  transfers between devices with their start and end apart: 34 -> 21, of which waited for: 17 -> 15; matrix products, arithmetic and copies ran while one was open for 0% -> 0% of each run, Pallas kernels for 7% -> 3%
where the time goes in v3:
time: 94.1 us; the launch traced here: 93.9 us
  waiting for transfers between devices  48.9 us (52%)
  starting transfers between devices  21.8 us (23%)
  blocking collectives  12.6 us (13%)
  Pallas kernels  6.85 us (7%)
  local copies, waits for them, and re-layouts  2.74 us (3%)
    ppermute x21, waiting for transfers between devices, swap(): return lax.ppermute(x, axis, [(i, i ^ mask) for i in range(size)])  48.9 us
    ppermute x21, starting transfers between devices, swap(): return lax.ppermute(x, axis, [(i, i ^ mask) for i in range(size)])  21.8 us
    all_to_all x1, blocking collectives, results(): peaks = lax.all_to_all(peak, ('tok', 'blk'), 0, 0, tiled=True)  12.6 us
    pallas_call x9, Pallas kernels, call(): pl.pallas_call(kernel, out_shape=outs, in_specs=specs, out_specs=out_spec...  6.85 us
    unnamed x8, local copies, waits for them, and re-layouts  2.74 us
  transfers between devices with their start and end apart: 21, of which 15 were waited for; matrix products, arithmetic and copies ran while one was open for 0% of the time, Pallas kernels for 3%

profile of v3, /device:TPU:0, one launch (start us, length us, event | category | flops | bytes accessed | tf_op | source)
XLA Modules:
  0.0 93.9 jit_solution(7752496424342714183)
XLA Ops:
  1.4 1.2 %copy-done = bf16[16,29568]{1,0:T(8,128)(2,1)S(1)} copy-done((bf16[16,29568]{1,0:T(8,128)(2,1)S(1)}, bf16[16,29568]{1,0:T(8,128)(2,1)}, u32[]{:S(2)}) %copy-start) | copy-done | bytes 946200
  3.6 1.5 %shard_map.59 = (bf16[112,16,128]{2,1,0:T(8,128)(2,1)S(1)}, bf16[112,16,128]{2,1,0:T(8,128)(2,1)S(1)}, bf16[160,16,128]{2,1,0:T(8,128)(2,1)S(1)}, bf16[160,16,12...) custom-call(s32[2]{0:T(128)S(1)} %pad_add_fusion.1.pos, s32[8,64]{1,0:T(8,128)S(1)} %get-tuple-element.47.cols, ...), custom_call_target="tpu_custom_call" | custom-call | flops 1 | bytes 1 | tf_op jit(solution)/shard_map/pallas_call | solution.py:32
  5.0 3.0 %collective-permute-start.1 = (bf16[160,16,128]{2,1,0:T(8,128)(2,1)S(1)}, bf16[160,16,128]{2,1,0:T(8,128)(2,1)S(1)}, u32[]{:S(2)}, u32[]{:S(2)}) collective-permute-start(bf16[160,16,128]{2,1,0:T(8,128)(2,1)S(1)} %get-tuple-element.44), channel_id=1, source_target_pairs={{0,2},{1,3},{2,0},{3,1},{4,6},{5,7},{6,4},{7,5},{8,10},{9,11},{10,... | collective-permute-start | bytes 1966088 | tf_op jit(solution)/shard_map/ppermute | solution.py:24
  8.0 1.5 %collective-permute-start.2 = (bf16[160,16,128]{2,1,0:T(8,128)(2,1)S(1)}, bf16[160,16,128]{2,1,0:T(8,128)(2,1)S(1)}, u32[]{:S(2)}, u32[]{:S(2)}) collective-permute-start(bf16[160,16,128]{2,1,0:T(8,128)(2,1)S(1)} %get-tuple-element.45), channel_id=1, source_target_pairs={{0,4},{1,5},{2,6},{3,7},{4,0},{5,1},{6,2},{7,3},{8,12},{9,13},{10,... | collective-permute-start | bytes 1966088 | tf_op jit(solution)/shard_map/ppermute | solution.py:24
  10.5 2.1 %collective-permute-start.4 = (bf16[64,16,128]{2,1,0:T(8,128)(2,1)S(1)}, bf16[64,16,128]{2,1,0:T(8,128)(2,1)S(1)}, u32[]{:S(2)}, u32[]{:S(2)}) collective-permute-start(bf16[64,16,128]{2,1,0:T(8,128)(2,1)S(1)} %get-tuple-element.49), channel_id=1, source_target_pairs={{0,8},{8,0},{16,24},{24,16},{1,9},{9,1},{17,25},{25,17},{2,10},{10... | collective-permute-start | bytes 786440 | tf_op jit(solution)/shard_map/ppermute | solution.py:24
  12.6 7.0 %collective-permute-done.4.refs_1_ = bf16[64,16,128]{2,1,0:T(8,128)(2,1)S(1)} collective-permute-done((bf16[64,16,128]{2,1,0:T(8,128)(2,1)S(1)}, bf16[64,16,128]{2,1,0:T(8,128)(2,1)S(1)}, u32[]{:S(2)}, u32[]{:S(2)}) %collective-permute-start.4) | collective-permute-done | bytes 262176 | tf_op jit(solution)/shard_map/ppermute | solution.py:24
  20.2 3.4 %collective-permute-done.1.refs_2_ = bf16[160,16,128]{2,1,0:T(8,128)(2,1)S(1)} collective-permute-done((bf16[160,16,128]{2,1,0:T(8,128)(2,1)S(1)}, bf16[160,16,128]{2,1,0:T(8,128)(2,1)S(1)}, u32[]{:S(2)}, u32[]{:S(2)}) %collective-permute-start.1) | collective-permute-done | bytes 655392 | tf_op jit(solution)/shard_map/ppermute | solution.py:24
  23.6 14.7 %collective-permute-done.2.refs_4_ = bf16[160,16,128]{2,1,0:T(8,128)(2,1)S(1)} collective-permute-done((bf16[160,16,128]{2,1,0:T(8,128)(2,1)S(1)}, bf16[160,16,128]{2,1,0:T(8,128)(2,1)S(1)}, u32[]{:S(2)}, u32[]{:S(2)}) %collective-permute-start.2) | collective-permute-done | bytes 655392 | tf_op jit(solution)/shard_map/ppermute | solution.py:24
  38.8 1.6 %collective-permute-done.5.refs_3_ = bf16[160,16,128]{2,1,0:T(8,128)(2,1)S(1)} collective-permute-done((bf16[160,16,128]{2,1,0:T(8,128)(2,1)S(1)}, bf16[160,16,128]{2,1,0:T(8,128)(2,1)S(1)}, u32[]{:S(2)}, u32[]{:S(2)}) %collective-permute-start.5) | collective-permute-done | bytes 655392 | tf_op jit(solution)/shard_map/ppermute | solution.py:24
  42.3 1.7 %shard_map.62 = (f32[12,128,128]{2,1,0:T(8,128)S(1)}, f32[12,128,128]{2,1,0:T(8,128)S(1)}, bf16[12,128,128]{2,1,0:T(8,128)(2,1)S(1)}, bf16[12,128,128]{2,1,0:T(8...) custom-call(s32[2]{0:T(128)S(1)} %pad_add_fusion.1.pos, ...), custom_call_target="tpu_custom_call" | custom-call | flops 1 | bytes 1 | tf_op jit(solution)/shard_map/pallas_call | solution.py:32
  44.0 1.6 %collective-permute-start.8 = (bf16[12,128,128]{2,1,0:T(8,128)(2,1)S(1)}, bf16[12,128,128]{2,1,0:T(8,128)(2,1)S(1)}, u32[]{:S(2)}, u32[]{:S(2)}) collective-permute-start(bf16[12,128,128]{2,1,0:T(8,128)(2,1)S(1)} %get-tuple-element.55), channel_id=1, source_target_pairs={{0,8},{8,0},{16,24},{24,16},{1,9},{9,1},{17,25},{25,17},{2,10},{10... | collective-permute-start | bytes 1179656 | tf_op jit(solution)/shard_map/ppermute | solution.py:24
  45.6 2.6 %collective-permute-start.14 = (bf16[12,128,128]{2,1,0:T(8,128)(2,1)S(1)}, bf16[12,128,128]{2,1,0:T(8,128)(2,1)S(1)}, u32[]{:S(2)}, u32[]{:S(2)}) collective-permute-start(bf16[12,128,128]{2,1,0:T(8,128)(2,1)S(1)} %get-tuple-element.71), channel_id=1, source_target_pairs={{0,16},{8,24},{16,0},{24,8},{1,17},{9,25},{17,1},{25,9},{2,18},{10... | collective-permute-start | bytes 1179656 | tf_op jit(solution)/shard_map/ppermute | solution.py:24
  48.2 1.2 %collective-permute-start.10 = (bf16[32,16,128]{2,1,0:T(8,128)(2,1)S(1)}, bf16[32,16,128]{2,1,0:T(8,128)(2,1)S(1)}, u32[]{:S(2)}, u32[]{:S(2)}) collective-permute-start(bf16[32,16,128]{2,1,0:T(8,128)(2,1)S(1)} %get-tuple-element.63), channel_id=1, source_target_pairs={{0,2},{1,3},{2,0},{3,1},{4,6},{5,7},{6,4},{7,5},{8,10},{9,11},{10,... | collective-permute-start | bytes 393224 | tf_op jit(solution)/shard_map/ppermute | solution.py:24
  50.3 1.4 %collective-permute-start.12 = (bf16[32,16,128]{2,1,0:T(8,128)(2,1)S(1)}, bf16[32,16,128]{2,1,0:T(8,128)(2,1)S(1)}, u32[]{:S(2)}, u32[]{:S(2)}) collective-permute-start(bf16[32,16,128]{2,1,0:T(8,128)(2,1)S(1)} %get-tuple-element.65), channel_id=1, source_target_pairs={{0,6},{1,7},{2,4},{3,5},{4,2},{5,3},{6,0},{7,1},{8,14},{9,15},{10,... | collective-permute-start | bytes 393224 | tf_op jit(solution)/shard_map/ppermute | solution.py:24
  51.7 2.8 %collective-permute-done.10.refs_2_ = bf16[32,16,128]{2,1,0:T(8,128)(2,1)S(1)} collective-permute-done((bf16[32,16,128]{2,1,0:T(8,128)(2,1)S(1)}, bf16[32,16,128]{2,1,0:T(8,128)(2,1)S(1)}, u32[]{:S(2)}, u32[]{:S(2)}) %collective-permute-start.10) | collective-permute-done | bytes 131104 | tf_op jit(solution)/shard_map/ppermute | solution.py:24
  54.5 1.8 %collective-permute-done.11.refs_4_ = bf16[32,16,128]{2,1,0:T(8,128)(2,1)S(1)} collective-permute-done((bf16[32,16,128]{2,1,0:T(8,128)(2,1)S(1)}, bf16[32,16,128]{2,1,0:T(8,128)(2,1)S(1)}, u32[]{:S(2)}, u32[]{:S(2)}) %collective-permute-start.11) | collective-permute-done | bytes 131104 | tf_op jit(solution)/shard_map/ppermute | solution.py:24
  56.3 1.6 %collective-permute-done.12.refs_6_ = bf16[32,16,128]{2,1,0:T(8,128)(2,1)S(1)} collective-permute-done((bf16[32,16,128]{2,1,0:T(8,128)(2,1)S(1)}, bf16[32,16,128]{2,1,0:T(8,128)(2,1)S(1)}, u32[]{:S(2)}, u32[]{:S(2)}) %collective-permute-start.12) | collective-permute-done | bytes 131104 | tf_op jit(solution)/shard_map/ppermute | solution.py:24
  58.3 6.0 %collective-permute-done.8.got = bf16[12,128,128]{2,1,0:T(8,128)(2,1)S(1)} collective-permute-done((bf16[12,128,128]{2,1,0:T(8,128)(2,1)S(1)}, bf16[12,128,128]{2,1,0:T(8,128)(2,1)S(1)}, u32[]{:S(2)}, u32[]{:S(2)}) %collective-permute-start.8) | collective-permute-done | bytes 393248 | tf_op jit(solution)/shard_map/ppermute | solution.py:24
  65.3 2.8 %collective-permute-start.15 = (bf16[6,128,128]{2,1,0:T(8,128)(2,1)S(1)}, bf16[6,128,128]{2,1,0:T(8,128)(2,1)S(1)}, u32[]{:S(2)}, u32[]{:S(2)}) collective-permute-start(bf16[6,128,128]{2,1,0:T(8,128)(2,1)S(1)} %get-tuple-element.73), channel_id=1, source_target_pairs={{0,8},{8,0},{16,24},{24,16},{1,9},{9,1},{17,25},{25,17},{2,10},{10... | collective-permute-start | bytes 589832 | tf_op jit(solution)/shard_map/ppermute | solution.py:24
  69.7 4.6 %collective-permute-done.19.refs_9_ = bf16[8,128,128]{2,1,0:T(8,128)(2,1)S(1)} collective-permute-done((bf16[8,128,128]{2,1,0:T(8,128)(2,1)S(1)}, bf16[8,128,128]{2,1,0:T(8,128)(2,1)S(1)}, u32[]{:S(2)}, u32[]{:S(2)}) %collective-permute-start.19) | collective-permute-done | bytes 262176 | tf_op jit(solution)/shard_map/ppermute | solution.py:24
  74.3 1.0 %shard_map.66 = (f32[4,128,128]{2,1,0:T(8,128)S(1)}, f32[4,128,128]{2,1,0:T(8,128)S(1)}) custom-call(s32[2]{0:T(128)S(1)} %pad_add_fusion.1.pos, bf16[16,16,128]{2,1,0:T(8,128)(2,1)S(1)} %get-tuple-element.76.refs_0_, bf16[16,16,128]{2,1,0:T(8,128)(2,1)S(1)} %collective-permute-done.13.refs_1_, bf16[32,16,128]{2,1,0:T(8,128)(2,1)S(1)} %collective-permute-done.10.refs_2_, ...), custom_call_target="tpu_custom_call" | custom-call | flops 1 | bytes 1 | tf_op jit(solution)/shard_map/pallas_call | solution.py:32
  75.3 2.4 %collective-permute-done.15.refs_3_ = bf16[6,128,128]{2,1,0:T(8,128)(2,1)S(1)} collective-permute-done((bf16[6,128,128]{2,1,0:T(8,128)(2,1)S(1)}, bf16[6,128,128]{2,1,0:T(8,128)(2,1)S(1)}, u32[]{:S(2)}, u32[]{:S(2)}) %collective-permute-start.15) | collective-permute-done | bytes 196640 | tf_op jit(solution)/shard_map/ppermute | solution.py:24
  77.9 2.6 %collective-permute-start.20 = (f32[4,128,128]{2,1,0:T(8,128)S(1)}, f32[4,128,128]{2,1,0:T(8,128)S(1)}, u32[]{:S(2)}, u32[]{:S(2)}) collective-permute-start(f32[4,128,128]{2,1,0:T(8,128)S(1)} %get-tuple-element.81), channel_id=1, source_target_pairs={{0,16},{8,24},{16,0},{24,8},{1,17},{9,25},{17,1},{25,9},{2,18},{10... | collective-permute-start | bytes 786440 | tf_op jit(solution)/shard_map/ppermute | solution.py:24
  80.6 12.6 %all_to_all.11 = f32[32,1,128]{2,1,0:T(1,128)S(1)} all-to-all(f32[32,1,128]{2,1,0:T(1,128)S(1)} %bitcast.7), channel_id=1, replica_groups=mesh['tok'=4,'blk'=8] {'tok','blk'}, dimensions={0} | all-to-all | bytes 32768 | tf_op jit(solution)/shard_map/all_to_all | solution.py:355
  (38 shorter events, 10.5 us)
Async XLA Ops:
  0.6 0.7 copy-start.2
  1.4 1.2 %copy-start = (bf16[16,29568]{1,0:T(8,128)(2,1)S(1)}, bf16[16,29568]{1,0:T(8,128)(2,1)}, u32[]{:S(2)}) copy-start(bf16[16,29568]{1,0:T(8,128)(2,1)} %grad.5) | copy-start | bytes 2838532
  2.6 0.9 %copy-start.1 = (bf16[128,1024]{1,0:T(8,128)(2,1)S(1)}, bf16[128,1024]{1,0:T(8,128)(2,1)}, u32[]{:S(2)}) copy-start(bf16[128,1024]{1,0:T(8,128)(2,1)} %refs_0_.1) | copy-start | bytes 786436
  5.0 18.6 %collective-permute-start.1 = (bf16[160,16,128]{2,1,0:T(8,128)(2,1)S(1)}, bf16[160,16,128]{2,1,0:T(8,128)(2,1)S(1)}, u32[]{:S(2)}, u32[]{:S(2)}) collective-permute-start(bf16[160,16,128]{2,1,0:T(8,128)(2,1)S(1)} %get-tuple-element.44), channel_id=1, source_target_pairs={{0,2},{1,3},{2,0},{3,1},{4,6},{5,7},{6,4},{7,5},{8,10},{9,11},{10,... | collective-permute-start | bytes 1966088 | tf_op jit(solution)/shard_map/ppermute | solution.py:24
  8.0 30.2 %collective-permute-start.2 = (bf16[160,16,128]{2,1,0:T(8,128)(2,1)S(1)}, bf16[160,16,128]{2,1,0:T(8,128)(2,1)S(1)}, u32[]{:S(2)}, u32[]{:S(2)}) collective-permute-start(bf16[160,16,128]{2,1,0:T(8,128)(2,1)S(1)} %get-tuple-element.45), channel_id=1, source_target_pairs={{0,4},{1,5},{2,6},{3,7},{4,0},{5,1},{6,2},{7,3},{8,12},{9,13},{10,... | collective-permute-start | bytes 1966088 | tf_op jit(solution)/shard_map/ppermute | solution.py:24
  9.6 28.7 %collective-permute-start.3 = (bf16[160,16,128]{2,1,0:T(8,128)(2,1)S(1)}, bf16[160,16,128]{2,1,0:T(8,128)(2,1)S(1)}, u32[]{:S(2)}, u32[]{:S(2)}) collective-permute-start(bf16[160,16,128]{2,1,0:T(8,128)(2,1)S(1)} %get-tuple-element.46), channel_id=1, source_target_pairs={{0,6},{1,7},{2,4},{3,5},{4,2},{5,3},{6,0},{7,1},{8,14},{9,15},{10,... | collective-permute-start | bytes 1966088 | tf_op jit(solution)/shard_map/ppermute | solution.py:24
  9.6 10.6 %collective-permute-start = (bf16[112,16,128]{2,1,0:T(8,128)(2,1)S(1)}, bf16[112,16,128]{2,1,0:T(8,128)(2,1)S(1)}, u32[]{:S(2)}, u32[]{:S(2)}) collective-permute-start(bf16[112,16,128]{2,1,0:T(8,128)(2,1)S(1)} %get-tuple-element.43), channel_id=1, source_target_pairs={{0,1},{1,0},{2,3},{3,2},{4,5},{5,4},{6,7},{7,6},{8,9},{9,8},{10,11... | collective-permute-start | bytes 1376264 | tf_op jit(solution)/shard_map/ppermute | solution.py:24
  10.5 9.1 %collective-permute-start.4 = (bf16[64,16,128]{2,1,0:T(8,128)(2,1)S(1)}, bf16[64,16,128]{2,1,0:T(8,128)(2,1)S(1)}, u32[]{:S(2)}, u32[]{:S(2)}) collective-permute-start(bf16[64,16,128]{2,1,0:T(8,128)(2,1)S(1)} %get-tuple-element.49), channel_id=1, source_target_pairs={{0,8},{8,0},{16,24},{24,16},{1,9},{9,1},{17,25},{25,17},{2,10},{10... | collective-permute-start | bytes 786440 | tf_op jit(solution)/shard_map/ppermute | solution.py:24
  38.3 2.1 %collective-permute-start.5 = (bf16[160,16,128]{2,1,0:T(8,128)(2,1)S(1)}, bf16[160,16,128]{2,1,0:T(8,128)(2,1)S(1)}, u32[]{:S(2)}, u32[]{:S(2)}) collective-permute-start(bf16[160,16,128]{2,1,0:T(8,128)(2,1)S(1)} %collective-permute-done.1.refs_2_), channel_id=1, source_target_pairs={{0,1},{1,0},{2,3},{3,2},{4,5},{5,4},{6,7},{7,6},{8,9},{9,8},{10,11... | collective-permute-start | bytes 1966088 | tf_op jit(solution)/shard_map/ppermute | solution.py:24
  38.3 3.0 %collective-permute-start.6 = (bf16[160,16,128]{2,1,0:T(8,128)(2,1)S(1)}, bf16[160,16,128]{2,1,0:T(8,128)(2,1)S(1)}, u32[]{:S(2)}, u32[]{:S(2)}) collective-permute-start(bf16[160,16,128]{2,1,0:T(8,128)(2,1)S(1)} %collective-permute-done.2.refs_4_), channel_id=1, source_target_pairs={{0,1},{1,0},{2,3},{3,2},{4,5},{5,4},{6,7},{7,6},{8,9},{9,8},{10,11... | collective-permute-start | bytes 1966088 | tf_op jit(solution)/shard_map/ppermute | solution.py:24
  38.8 3.5 %collective-permute-start.7 = (bf16[160,16,128]{2,1,0:T(8,128)(2,1)S(1)}, bf16[160,16,128]{2,1,0:T(8,128)(2,1)S(1)}, u32[]{:S(2)}, u32[]{:S(2)}) collective-permute-start(bf16[160,16,128]{2,1,0:T(8,128)(2,1)S(1)} %collective-permute-done.3.refs_6_), channel_id=1, source_target_pairs={{0,1},{1,0},{2,3},{3,2},{4,5},{5,4},{6,7},{7,6},{8,9},{9,8},{10,11... | collective-permute-start | bytes 1966088 | tf_op jit(solution)/shard_map/ppermute | solution.py:24
  44.0 20.3 %collective-permute-start.8 = (bf16[12,128,128]{2,1,0:T(8,128)(2,1)S(1)}, bf16[12,128,128]{2,1,0:T(8,128)(2,1)S(1)}, u32[]{:S(2)}, u32[]{:S(2)}) collective-permute-start(bf16[12,128,128]{2,1,0:T(8,128)(2,1)S(1)} %get-tuple-element.55), channel_id=1, source_target_pairs={{0,8},{8,0},{16,24},{24,16},{1,9},{9,1},{17,25},{25,17},{2,10},{10... | collective-permute-start | bytes 1179656 | tf_op jit(solution)/shard_map/ppermute | solution.py:24
  45.6 19.6 %collective-permute-start.14 = (bf16[12,128,128]{2,1,0:T(8,128)(2,1)S(1)}, bf16[12,128,128]{2,1,0:T(8,128)(2,1)S(1)}, u32[]{:S(2)}, u32[]{:S(2)}) collective-permute-start(bf16[12,128,128]{2,1,0:T(8,128)(2,1)S(1)} %get-tuple-element.71), channel_id=1, source_target_pairs={{0,16},{8,24},{16,0},{24,8},{1,17},{9,25},{17,1},{25,9},{2,18},{10... | collective-permute-start | bytes 1179656 | tf_op jit(solution)/shard_map/ppermute | solution.py:24
  48.2 2.1 %collective-permute-start.13 = (bf16[16,16,128]{2,1,0:T(8,128)(2,1)S(1)}, bf16[16,16,128]{2,1,0:T(8,128)(2,1)S(1)}, u32[]{:S(2)}, u32[]{:S(2)}) collective-permute-start(bf16[16,16,128]{2,1,0:T(8,128)(2,1)S(1)} %get-tuple-element.66), channel_id=1, source_target_pairs={{0,1},{1,0},{2,3},{3,2},{4,5},{5,4},{6,7},{7,6},{8,9},{9,8},{10,11... | collective-permute-start | bytes 196616 | tf_op jit(solution)/shard_map/ppermute | solution.py:24
  48.2 6.3 %collective-permute-start.10 = (bf16[32,16,128]{2,1,0:T(8,128)(2,1)S(1)}, bf16[32,16,128]{2,1,0:T(8,128)(2,1)S(1)}, u32[]{:S(2)}, u32[]{:S(2)}) collective-permute-start(bf16[32,16,128]{2,1,0:T(8,128)(2,1)S(1)} %get-tuple-element.63), channel_id=1, source_target_pairs={{0,2},{1,3},{2,0},{3,1},{4,6},{5,7},{6,4},{7,5},{8,10},{9,11},{10,... | collective-permute-start | bytes 393224 | tf_op jit(solution)/shard_map/ppermute | solution.py:24
  49.4 6.8 %collective-permute-start.11 = (bf16[32,16,128]{2,1,0:T(8,128)(2,1)S(1)}, bf16[32,16,128]{2,1,0:T(8,128)(2,1)S(1)}, u32[]{:S(2)}, u32[]{:S(2)}) collective-permute-start(bf16[32,16,128]{2,1,0:T(8,128)(2,1)S(1)} %get-tuple-element.64), channel_id=1, source_target_pairs={{0,4},{1,5},{2,6},{3,7},{4,0},{5,1},{6,2},{7,3},{8,12},{9,13},{10,... | collective-permute-start | bytes 393224 | tf_op jit(solution)/shard_map/ppermute | solution.py:24
  50.3 7.6 %collective-permute-start.12 = (bf16[32,16,128]{2,1,0:T(8,128)(2,1)S(1)}, bf16[32,16,128]{2,1,0:T(8,128)(2,1)S(1)}, u32[]{:S(2)}, u32[]{:S(2)}) collective-permute-start(bf16[32,16,128]{2,1,0:T(8,128)(2,1)S(1)} %get-tuple-element.65), channel_id=1, source_target_pairs={{0,6},{1,7},{2,4},{3,5},{4,2},{5,3},{6,0},{7,1},{8,14},{9,15},{10,... | collective-permute-start | bytes 393224 | tf_op jit(solution)/shard_map/ppermute | solution.py:24
  57.9 10.3 %collective-permute-start.16 = (bf16[32,16,128]{2,1,0:T(8,128)(2,1)S(1)}, bf16[32,16,128]{2,1,0:T(8,128)(2,1)S(1)}, u32[]{:S(2)}, u32[]{:S(2)}) collective-permute-start(bf16[32,16,128]{2,1,0:T(8,128)(2,1)S(1)} %collective-permute-done.10.refs_2_), channel_id=1, source_target_pairs={{0,1},{1,0},{2,3},{3,2},{4,5},{5,4},{6,7},{7,6},{8,9},{9,8},{10,11... | collective-permute-start | bytes 393224 | tf_op jit(solution)/shard_map/ppermute | solution.py:24
  57.9 16.4 %collective-permute-start.19 = (bf16[8,128,128]{2,1,0:T(8,128)(2,1)S(1)}, bf16[8,128,128]{2,1,0:T(8,128)(2,1)S(1)}, u32[]{:S(2)}, u32[]{:S(2)}) collective-permute-start(bf16[8,128,128]{2,1,0:T(8,128)(2,1)S(1)} %get-tuple-element.78), channel_id=1, source_target_pairs={{0,8},{8,0},{16,24},{24,16},{1,9},{9,1},{17,25},{25,17},{2,10},{10... | collective-permute-start | bytes 786440 | tf_op jit(solution)/shard_map/ppermute | solution.py:24
  64.4 10.8 %collective-permute-start.9 = (bf16[6,128,128]{2,1,0:T(8,128)(2,1)S(1)}, bf16[6,128,128]{2,1,0:T(8,128)(2,1)S(1)}, u32[]{:S(2)}, u32[]{:S(2)}) collective-permute-start(bf16[6,128,128]{2,1,0:T(8,128)(2,1)S(1)} %get-tuple-element.57), channel_id=1, source_target_pairs={{0,16},{8,24},{16,0},{24,8},{1,17},{9,25},{17,1},{25,9},{2,18},{10... | collective-permute-start | bytes 589832 | tf_op jit(solution)/shard_map/ppermute | solution.py:24
  65.3 12.3 %collective-permute-start.15 = (bf16[6,128,128]{2,1,0:T(8,128)(2,1)S(1)}, bf16[6,128,128]{2,1,0:T(8,128)(2,1)S(1)}, u32[]{:S(2)}, u32[]{:S(2)}) collective-permute-start(bf16[6,128,128]{2,1,0:T(8,128)(2,1)S(1)} %get-tuple-element.73), channel_id=1, source_target_pairs={{0,8},{8,0},{16,24},{24,16},{1,9},{9,1},{17,25},{25,17},{2,10},{10... | collective-permute-start | bytes 589832 | tf_op jit(solution)/shard_map/ppermute | solution.py:24
  68.1 1.3 %collective-permute-start.17 = (bf16[32,16,128]{2,1,0:T(8,128)(2,1)S(1)}, bf16[32,16,128]{2,1,0:T(8,128)(2,1)S(1)}, u32[]{:S(2)}, u32[]{:S(2)}) collective-permute-start(bf16[32,16,128]{2,1,0:T(8,128)(2,1)S(1)} %collective-permute-done.11.refs_4_), channel_id=1, source_target_pairs={{0,1},{1,0},{2,3},{3,2},{4,5},{5,4},{6,7},{7,6},{8,9},{9,8},{10,11... | collective-permute-start | bytes 393224 | tf_op jit(solution)/shard_map/ppermute | solution.py:24
  68.1 1.5 %collective-permute-start.18 = (bf16[32,16,128]{2,1,0:T(8,128)(2,1)S(1)}, bf16[32,16,128]{2,1,0:T(8,128)(2,1)S(1)}, u32[]{:S(2)}, u32[]{:S(2)}) collective-permute-start(bf16[32,16,128]{2,1,0:T(8,128)(2,1)S(1)} %collective-permute-done.12.refs_6_), channel_id=1, source_target_pairs={{0,1},{1,0},{2,3},{3,2},{4,5},{5,4},{6,7},{7,6},{8,9},{9,8},{10,11... | collective-permute-start | bytes 393224 | tf_op jit(solution)/shard_map/ppermute | solution.py:24
  77.9 15.3 %collective-permute-start.20 = (f32[4,128,128]{2,1,0:T(8,128)S(1)}, f32[4,128,128]{2,1,0:T(8,128)S(1)}, u32[]{:S(2)}, u32[]{:S(2)}) collective-permute-start(f32[4,128,128]{2,1,0:T(8,128)S(1)} %get-tuple-element.81), channel_id=1, source_target_pairs={{0,16},{8,24},{16,0},{24,8},{1,17},{9,25},{17,1},{25,9},{2,18},{10... | collective-permute-start | bytes 786440 | tf_op jit(solution)/shard_map/ppermute | solution.py:24
  (1 other events, 0.7 us)

commit v4 on v3

--- a/solution.py
+++ b/solution.py
@@ -40,11 +40,9 @@
     )(*args)
 
 
-def pack_kernel(slots, masks, acts_width, extra, pos, cols, grad, *refs):
+def pack_kernel(slots, masks, acts_width, pos, cols, grad, *refs):
     me = pos[0]
-    acts = refs[:1] if acts_width else ()
-    others = refs[len(acts) : len(refs) - len(masks)]
-    outs = refs[len(refs) - len(masks) :]
+    acts, outs = refs[: -len(masks)], refs[-len(masks) :]
     for acts_ref in acts:
         for row in range(acts_width // BLOCK):
             block = acts_ref[:, row * BLOCK : (row + 1) * BLOCK].T
@@ -59,29 +57,23 @@
                 start = pl.multiple_of(cols[dest, slot] * BLOCK, BLOCK)
                 out[at] = grad[:, pl.ds(start, BLOCK)]
                 at += 1
-            for other in others:
-                out[at : at + extra] = other[pl.ds(dest * extra, extra)]
-                at += extra
 
 
 def owner_masks():
     return [(0,), (1,)] + [(m, m + 1) for m in range(2, lax.axis_size("blk"), 2)]
 
 
-def pack(out_grad, cols, pos, slots, acts=None, others=()):
+def pack(out_grad, cols, pos, slots, acts=None):
     masks = owner_masks()
     width = 0 if acts is None else acts.shape[1]
-    extra = others[0].shape[0] // lax.axis_size("blk") if others else 0
-    count = len(slots) + extra * len(others)
-    more = list(others) if acts is None else [acts]
-    return call(
-        functools.partial(pack_kernel, slots, masks, width, extra),
-        [
-            jax.ShapeDtypeStruct((width // ROWS + len(d) * count, ROWS, BLOCK), out_grad.dtype)
+    return call(
+        functools.partial(pack_kernel, slots, masks, width),
+        [
+            jax.ShapeDtypeStruct((width // ROWS + len(d) * len(slots), ROWS, BLOCK), out_grad.dtype)
             for d in masks
         ],
-        [pos, cols, out_grad] + more,
-        [SMEM, SMEM] + [VMEM] * (1 + len(more)),
+        [pos, cols, out_grad] + ([] if acts is None else [acts]),
+        [SMEM, SMEM] + [VMEM] * (1 if acts is None else 2),
         [VMEM] * len(masks),
     )
 
@@ -122,18 +114,18 @@
     return [unit for unit in units if not unit & mask]
 
 
-def product_kernel(plan, toks, bounds, first, spare, pos, rows, *refs):
+def product_kernel(plan, toks, bounds, first, stride, pos, rows, *refs):
     copies_of, inputs = plan
     srcs = refs[:inputs]
     *outs, acts_all, grad_all, sem = refs[inputs:]
-    keeps, sends = outs[: len(bounds)], outs[len(bounds) : 2 * len(bounds)]
-    spares = outs[2 * len(bounds) :]
-    share = bounds[-1][1]
+    keeps, sends = outs[: len(bounds)], outs[len(bounds) :]
+    begin = bounds[0][0]
+    share = bounds[-1][1] - begin
     me, tok = pos[0], pos[1]
     copies = []
-    for n, (which, src, begin, size, peer) in enumerate(copies_of):
+    for n, (which, src, offset, size, peer) in enumerate(copies_of):
         at = 0 if peer is None else me ^ peer
-        from_ref = srcs[src].at[pl.ds(begin, size)]
+        from_ref = srcs[src].at[pl.ds(offset, size)]
         if which == "acts":
             dst = acts_all.at[pl.ds(pl.multiple_of(at * size, size), size)]
         elif peer is None:
@@ -146,25 +138,20 @@
         copy.start()
     for copy in copies:
         copy.wait()
-    for peer in range(toks if spares else 0):
-        for k in range(spare):
-            row = rows[me, (tok ^ peer) * spare + k] * PER_BLOCK
-            block = acts_all[pl.ds(pl.multiple_of(row, PER_BLOCK), PER_BLOCK)]
-            spares[peer % 2][peer // 2 * spare + k] = block.reshape(BLOCK, BLOCK)
     for peer in range(toks):
         unit = tok ^ peer
         for k in range(share):
             slot = unit * share + k
-            row = rows[me, first + slot] * PER_BLOCK
+            row = rows[me, first + unit * stride + begin + k] * PER_BLOCK
             left = acts_all[pl.ds(pl.multiple_of(row, PER_BLOCK), PER_BLOCK)]
             prod = jnp.dot(
                 left.reshape(BLOCK, BLOCK), grad_all[slot], preferred_element_type=jnp.float32
             )
             for (lo, hi, mask), keep, send in zip(bounds, keeps, sends):
-                if lo <= k < hi:
+                if lo <= begin + k < hi:
                     out = send if peer & mask else keep
                     at = kept_units(range(toks), mask).index(peer & ~mask)
-                    out[at * (hi - lo) + k - lo] = prod.astype(out.dtype)
+                    out[at * (hi - lo) + begin + k - lo] = prod.astype(out.dtype)
 
 
 def gather_plan(owners, width, count, acts_from, grads_from):
@@ -192,22 +179,20 @@
     return buffers, copies
 
 
-def products(acts_from, grads_from, width, rows, pos, bounds, first, dtype, spare=0):
+def products(acts_from, grads_from, width, rows, pos, bounds, first, stride, dtype):
     owners, toks = lax.axis_size("blk"), lax.axis_size("tok")
-    count = toks * bounds[-1][1]
+    count = toks * (bounds[-1][1] - bounds[0][0])
     buffers, copies = gather_plan(owners, width, count, acts_from, grads_from)
     sizes = [toks // 2 * (hi - lo) for lo, hi, _ in bounds]
-    spares = 2 if spare else 0
     return call(
         functools.partial(
-            product_kernel, (copies, len(buffers)), toks, bounds, first, spare
+            product_kernel, (copies, len(buffers)), toks, bounds, first, stride
         ),
         [jax.ShapeDtypeStruct((n, BLOCK, BLOCK), jnp.float32) for n in sizes]
-        + [jax.ShapeDtypeStruct((n, BLOCK, BLOCK), dtype) for n in sizes]
-        + [jax.ShapeDtypeStruct((toks // 2 * spare, BLOCK, BLOCK), jnp.bfloat16)] * spares,
+        + [jax.ShapeDtypeStruct((n, BLOCK, BLOCK), dtype) for n in sizes],
         [pos, rows] + buffers,
         [SMEM, SMEM] + [ANY] * len(buffers),
-        [VMEM] * (2 * len(bounds) + spares),
+        [VMEM] * (2 * len(bounds)),
         [
             pltpu.VMEM((owners * width, ROWS, BLOCK), jnp.bfloat16),
             pltpu.VMEM((count, BLOCK, BLOCK), jnp.bfloat16),
@@ -216,68 +201,111 @@
     )
 
 
-def kept_pack_kernel(share, pos, cols, grad, *outs):
-    units = 2 * outs[0].shape[0] // share // cols.shape[0]
-    for peer in range(units):
+def kept_pack_kernel(share, mask, width, pos, cols, grad, acts, own, other):
+    half = own.shape[0] // share // cols.shape[0]
+    other[:width] = acts[:width]
+    for peer in range(2 * half):
         unit = pos[1] ^ peer
-        out = outs[peer % 2]
+        index = kept_units(range(2 * half), mask).index(peer & ~mask)
         for dest in range(cols.shape[0]):
+            at = (dest * half + index) * share
+            out, at = (other, at + width) if peer & mask else (own, at)
             for k in range(share):
                 start = pl.multiple_of(cols[dest, unit * share + k] * BLOCK, BLOCK)
-                at = (dest * (units // 2) + peer // 2) * share + k
-                out[at] = grad[:, pl.ds(start, BLOCK)]
-
-
-def kept_pack(out_grad, cols, pos, share):
+                out[at + k] = grad[:, pl.ds(start, BLOCK)]
+
+
+def kept_pack(out_grad, cols, pos, acts, width, share, mask):
     owners, toks = lax.axis_size("blk"), lax.axis_size("tok")
-    shape = (owners * (toks // 2) * share, ROWS, BLOCK)
-    return call(
-        functools.partial(kept_pack_kernel, share),
-        [jax.ShapeDtypeStruct(shape, out_grad.dtype)] * 2,
-        (pos, cols, out_grad),
-        [SMEM, SMEM, VMEM],
-        [VMEM] * 2,
-    )
-
-
-def kept_product_kernel(copies_of, inputs, share, pos, *refs):
+    count = owners * (toks // 2) * share
+    return call(
+        functools.partial(kept_pack_kernel, share, mask, width),
+        [jax.ShapeDtypeStruct((n, ROWS, BLOCK), out_grad.dtype) for n in (count, width + count)],
+        (pos, cols, out_grad, acts),
+        [SMEM, SMEM, VMEM, VMEM],
+        [VMEM] * 2,
+    )
+
+
+def kept_split_kernel(width, extra, masks, pos, own, other, *outs):
+    for out, dests in zip(outs, masks):
+        out[:width] = other[:width]
+        at = width
+        for mask in dests:
+            dest = pos[0] ^ mask
+            out[at : at + extra] = own[pl.ds(dest * extra, extra)]
+            out[at + extra : at + 2 * extra] = other[pl.ds(width + dest * extra, extra)]
+            at += 2 * extra
+
+
+def kept_split(own, other, pos, width):
+    masks = owner_masks()
+    extra = own.shape[0] // lax.axis_size("blk")
+    return call(
+        functools.partial(kept_split_kernel, width, extra, masks),
+        [
+            jax.ShapeDtypeStruct((width + 2 * extra * len(d), ROWS, BLOCK), own.dtype)
+            for d in masks
+        ],
+        (pos, own, other),
+        [SMEM, VMEM, VMEM],
+        [VMEM] * len(masks),
+    )
+
+
+def kept_product_kernel(copies_of, inputs, width, share, units, mask, pos, rows, *refs):
     srcs = refs[:inputs]
-    lefts = refs[inputs : inputs + 2]
-    keep, send, grad_all, sem = refs[inputs + 2 :]
+    keep, send, acts_all, grad_all, sem = refs[inputs:]
+    me, tok = pos[0], pos[1]
     copies = []
-    for n, (_, src, begin, size, peer) in enumerate(copies_of):
-        at = pl.multiple_of((pos[0] ^ peer) * ROWS, ROWS)
-        copies.append(
-            pltpu.make_async_copy(
-                srcs[src].at[pl.ds(begin, size)], grad_all.at[:, pl.ds(at, ROWS)], sem.at[n]
-            )
-        )
+    for n, (which, src, begin, size, peer) in enumerate(copies_of):
+        if which == "grad":
+            at = pl.multiple_of((me ^ peer) * ROWS, ROWS)
+            dst = grad_all.at[:, pl.ds(at, ROWS)]
+        else:
+            at = pl.multiple_of((me ^ peer) * width, width)
+            dst = acts_all.at[which, pl.ds(at, width)]
+        copies.append(pltpu.make_async_copy(srcs[src].at[pl.ds(begin, size)], dst, sem.at[n]))
     for copy in copies:
         copy.start()
     for copy in copies:
         copy.wait()
-    half = lefts[0].shape[0]
-    for k in range(half):
-        total = jnp.zeros((BLOCK, BLOCK), jnp.float32)
-        for part, left in enumerate(lefts):
-            total += jnp.dot(
-                left[k], grad_all[part * half + k], preferred_element_type=jnp.float32
-            )
-        unit, slot = divmod(k, share)
-        (send if unit % 2 else keep)[unit // 2 * share + slot] = total
-
-
-def kept_product(lefts, grads_from, pos, share):
+    half = len(units) * share
+    for index, unit in enumerate(units):
+        out = send if unit & mask else keep
+        at = kept_units(units, mask).index(unit & ~mask) * share
+        for slot in range(share):
+            row = rows[me, (tok ^ unit) * share + slot] * PER_BLOCK
+            total = jnp.zeros((BLOCK, BLOCK), jnp.float32)
+            for group in range(2):
+                left = acts_all[group, pl.ds(pl.multiple_of(row, PER_BLOCK), PER_BLOCK)]
+                total += jnp.dot(
+                    left.reshape(BLOCK, BLOCK),
+                    grad_all[group * half + index * share + slot],
+                    preferred_element_type=jnp.float32,
+                )
+            out[at + slot] = total
+
+
+def kept_product(from0, from2, rows, pos, width, share, units, mask):
     owners = lax.axis_size("blk")
-    half = lefts[0].shape[0]
-    buffers, copies = gather_plan(owners, 0, 2 * half, None, grads_from)
-    return call(
-        functools.partial(kept_product_kernel, copies, len(buffers), share),
+    half = len(units) * share
+    buffers = [buffer for buffer, _ in from0 + from2]
+    copies = []
+    for peer in range(owners):
+        copies.append((0, peer, 0, width, peer))
+        copies.append((1, owners + peer, 0, width, peer))
+        copies.append(("grad", owners + peer, from2[peer][1], 2 * half, peer))
+    return call(
+        functools.partial(
+            kept_product_kernel, copies, len(buffers), width, share, units, mask
+        ),
         [jax.ShapeDtypeStruct((half // 2, BLOCK, BLOCK), jnp.float32)] * 2,
-        [pos] + buffers + lefts,
-        [SMEM] + [ANY] * len(buffers) + [VMEM] * 2,
-        [VMEM] * 2,
-        [
+        [pos, rows] + buffers,
+        [SMEM, SMEM] + [ANY] * len(buffers),
+        [VMEM] * 2,
+        [
+            pltpu.VMEM((2, owners * width, ROWS, BLOCK), jnp.bfloat16),
             pltpu.VMEM((2 * half, BLOCK, BLOCK), jnp.bfloat16),
             pltpu.SemaphoreType.DMA((len(copies),)),
         ],
@@ -386,7 +414,7 @@
     if out_grad.shape[0] % ROWS:
         whole = lax.all_gather(acts.T, "blk", axis=0, tiled=True).reshape(-1, ROWS, BLOCK)
         keep0, keep1, send0, send1 = products(
-            whole, columns_plain(out_grad, cols, cands), width, rows, pos, bounds, ks, bf16
+            whole, columns_plain(out_grad, cols, cands), width, rows, pos, bounds, ks, cand_share, bf16
         )
         keep2, send2 = products(
             whole,
@@ -396,6 +424,7 @@
             pos,
             ((0, kept_share, 1),),
             0,
+            kept_share,
             f32,
         )
         row, peak = block_norms(
@@ -405,23 +434,27 @@
     else:
         buffers0 = pack(out_grad, cols, pos, cands, acts)
         cols = after(cols, buffers0[0])
-        kept = kept_pack(out_grad, cols, pos, kept_share)
+        own, other = kept_pack(out_grad, cols, pos, buffers0[0], width, kept_share, up[0])
         arrived0 = exchange(buffers0)
-        kept = [kept[0], swap(kept[1], "tok", 1)]
-        buffers2 = pack(out_grad, cols, pos, [], None, kept)
+        buffers2 = kept_split(own, swap(other, 'tok', up[0]), pos, width)
         from0 = forward(arrived0, len(cands), buffers2[0])
-        keep0, keep1, send0, send1, left, left_sent = products(
-            from0, from0, width, rows, pos, bounds, ks, bf16, kept_share
-        )
-        arrived2 = exchange(after(buffers2, keep1))
+        keep0, keep1, send0, send1 = products(from0, from0, width, rows, pos, bounds, ks, cand_share, bf16)
+        units = [kept_units(range(toks), order[0]) for order in orders]
+        step0 = swap(send0, 'tok', orders[0][0])
+        step1 = swap(send1, 'tok', orders[1][0])
+        arrived2 = exchange(buffers2)
+        keep0, send0 = add(keep0, step0, half, bf16, units[0], orders[0][1])
+        keep1 = after(keep1, send0)
+        keep1, send1 = add(keep1, step1, cand_share - half, bf16, units[1], orders[1][1])
         from2 = forward(arrived2, ks)
-        lefts = [left, swap(left_sent, "tok", 1)]
-        row, peak = block_norms(
-            halve(keep0, send0, half, orders[0]),
-            halve(after(keep1, *arrived2[2::2]), send1, cand_share - half, orders[1]),
-        )
-        keep2, send2 = kept_product(lefts, from2, pos, kept_share)
-        pair2 = halve(keep2, after(send2, row), kept_share, up[1:], range(0, toks, 2))
+        pair0 = halve(keep0, send0, half, orders[0][1:], units[0])
+        pair1 = halve(keep1, send1, cand_share - half, orders[1][1:], units[1])
+        from2[0] = (after(from2[0][0], send1), from2[0][1])
+        evens = kept_units(range(toks), up[0])
+        keep2, send2 = kept_product(from0, from2, rows, pos, width, kept_share, evens, up[1])
+        row, peak = block_norms(pair0, pair1)
+        send2 = after(send2, pair0[1], pair1[1])
+        pair2 = halve(keep2, send2, kept_share, up[1:], range(0, toks, 2))
 
     kept_grad, cand_score = results(row, peak, cand_share, pair2)
     return (kept_grad, cand_score)

time: 94.1 us -> 91.1 us (0.968)
  starting transfers between devices: 21.8 us -> 17.8 us
    ppermute x21 -> x20, starting transfers between devices: 21.8 us -> 17.8 us  [swap(): return lax.ppermute(x, axis, [(i, i ^ mask) for i in range(size)])]
    ppermute x21 -> x20, waiting for transfers between devices: 48.9 us -> 49.3 us  [swap(): return lax.ppermute(x, axis, [(i, i ^ mask) for i in range(size)])]
  transfers between devices with their start and end apart: 21 -> 20, of which waited for: 15 -> 8; matrix products, arithmetic and copies ran while one was open for 0% -> 0% of each run, Pallas kernels for 3% -> 6%
where the time goes in v4:
time: 91.1 us; the launch traced here: 90.9 us
  waiting for transfers between devices  49.3 us (54%)
  starting transfers between devices  17.8 us (20%)
  blocking collectives  12.7 us (14%)
  Pallas kernels  7.45 us (8%)
  local copies, waits for them, and re-layouts  2.74 us (3%)
    ppermute x20, waiting for transfers between devices, swap(): return lax.ppermute(x, axis, [(i, i ^ mask) for i in range(size)])  49.3 us
    ppermute x20, starting transfers between devices, swap(): return lax.ppermute(x, axis, [(i, i ^ mask) for i in range(size)])  17.8 us
    all_to_all x1, blocking collectives, results(): peaks = lax.all_to_all(peak, ('tok', 'blk'), 0, 0, tiled=True)  12.7 us
    pallas_call x9, Pallas kernels, call(): pl.pallas_call(kernel, out_shape=outs, in_specs=specs, out_specs=out_spec...  7.45 us
    unnamed x8, local copies, waits for them, and re-layouts  2.74 us
  transfers between devices with their start and end apart: 20, of which 8 were waited for; matrix products, arithmetic and copies ran while one was open for 0% of the time, Pallas kernels for 6%

profile of v4, /device:TPU:0, one launch (start us, length us, event | category | flops | bytes accessed | tf_op | source)
XLA Modules:
  0.0 90.9 jit_solution(17265929161217028285)
XLA Ops:
  1.4 1.2 %copy-done = bf16[16,29568]{1,0:T(8,128)(2,1)S(1)} copy-done((bf16[16,29568]{1,0:T(8,128)(2,1)S(1)}, bf16[16,29568]{1,0:T(8,128)(2,1)}, u32[]{:S(2)}) %copy-start) | copy-done | bytes 946200
  2.6 0.9 %copy-done.1 = bf16[128,1024]{1,0:T(8,128)(2,1)S(1)} copy-done((bf16[128,1024]{1,0:T(8,128)(2,1)S(1)}, bf16[128,1024]{1,0:T(8,128)(2,1)}, u32[]{:S(2)}) %copy-start.1) | copy-done | bytes 262168
  3.6 1.5 %shard_map.59 = (bf16[112,16,128]{2,1,0:T(8,128)(2,1)S(1)}, bf16[112,16,128]{2,1,0:T(8,128)(2,1)S(1)}, bf16[160,16,128]{2,1,0:T(8,128)(2,1)S(1)}, bf16[160,16,12...) custom-call(s32[2]{0:T(128)S(1)} %pad_add_fusion.1.pos, s32[8,64]{1,0:T(8,128)S(1)} %get-tuple-element.41.cols, ...), custom_call_target="tpu_custom_call" | custom-call | flops 1 | bytes 1 | tf_op jit(solution)/shard_map/pallas_call | solution.py:32
  5.0 3.0 %collective-permute-start.1 = (bf16[160,16,128]{2,1,0:T(8,128)(2,1)S(1)}, bf16[160,16,128]{2,1,0:T(8,128)(2,1)S(1)}, u32[]{:S(2)}, u32[]{:S(2)}) collective-permute-start(bf16[160,16,128]{2,1,0:T(8,128)(2,1)S(1)} %get-tuple-element.38), channel_id=1, source_target_pairs={{0,2},{1,3},{2,0},{3,1},{4,6},{5,7},{6,4},{7,5},{8,10},{9,11},{10,... | collective-permute-start | bytes 1966088 | tf_op jit(solution)/shard_map/ppermute | solution.py:24
  8.0 1.5 %collective-permute-start.2 = (bf16[160,16,128]{2,1,0:T(8,128)(2,1)S(1)}, bf16[160,16,128]{2,1,0:T(8,128)(2,1)S(1)}, u32[]{:S(2)}, u32[]{:S(2)}) collective-permute-start(bf16[160,16,128]{2,1,0:T(8,128)(2,1)S(1)} %get-tuple-element.39), channel_id=1, source_target_pairs={{0,4},{1,5},{2,6},{3,7},{4,0},{5,1},{6,2},{7,3},{8,12},{9,13},{10,... | collective-permute-start | bytes 1966088 | tf_op jit(solution)/shard_map/ppermute | solution.py:24
  9.6 0.9 shard_map.60
  10.5 2.1 %collective-permute-start.4 = (bf16[128,16,128]{2,1,0:T(8,128)(2,1)S(1)}, bf16[128,16,128]{2,1,0:T(8,128)(2,1)S(1)}, u32[]{:S(2)}, u32[]{:S(2)}) collective-permute-start(bf16[128,16,128]{2,1,0:T(8,128)(2,1)S(1)} %get-tuple-element.43), channel_id=1, source_target_pairs={{0,8},{8,0},{16,24},{24,16},{1,9},{9,1},{17,25},{25,17},{2,10},{10... | collective-permute-start | bytes 1572872 | tf_op jit(solution)/shard_map/ppermute | solution.py:24
  12.6 11.1 %collective-permute-done.4.other = bf16[128,16,128]{2,1,0:T(8,128)(2,1)S(1)} collective-permute-done((bf16[128,16,128]{2,1,0:T(8,128)(2,1)S(1)}, bf16[128,16,128]{2,1,0:T(8,128)(2,1)S(1)}, u32[]{:S(2)}, u32[]{:S(2)}) %collective-permute-start.4) | collective-permute-done | bytes 524320 | tf_op jit(solution)/shard_map/ppermute | solution.py:24
  23.6 0.7 shard_map.61
  24.4 13.9 %collective-permute-done.2.refs_4_ = bf16[160,16,128]{2,1,0:T(8,128)(2,1)S(1)} collective-permute-done((bf16[160,16,128]{2,1,0:T(8,128)(2,1)S(1)}, bf16[160,16,128]{2,1,0:T(8,128)(2,1)S(1)}, u32[]{:S(2)}, u32[]{:S(2)}) %collective-permute-start.2) | collective-permute-done | bytes 655392 | tf_op jit(solution)/shard_map/ppermute | solution.py:24
  39.3 1.2 %collective-permute-start.13 = (bf16[96,16,128]{2,1,0:T(8,128)(2,1)S(1)}, bf16[96,16,128]{2,1,0:T(8,128)(2,1)S(1)}, u32[]{:S(2)}, u32[]{:S(2)}) collective-permute-start(bf16[96,16,128]{2,1,0:T(8,128)(2,1)S(1)} %get-tuple-element.61), channel_id=1, source_target_pairs={{0,2},{1,3},{2,0},{3,1},{4,6},{5,7},{6,4},{7,5},{8,10},{9,11},{10,... | collective-permute-start | bytes 1179656 | tf_op jit(solution)/shard_map/ppermute | solution.py:24
  40.5 1.4 %collective-permute-start.14 = (bf16[96,16,128]{2,1,0:T(8,128)(2,1)S(1)}, bf16[96,16,128]{2,1,0:T(8,128)(2,1)S(1)}, u32[]{:S(2)}, u32[]{:S(2)}) collective-permute-start(bf16[96,16,128]{2,1,0:T(8,128)(2,1)S(1)} %get-tuple-element.62), channel_id=1, source_target_pairs={{0,4},{1,5},{2,6},{3,7},{4,0},{5,1},{6,2},{7,3},{8,12},{9,13},{10,... | collective-permute-start | bytes 1179656 | tf_op jit(solution)/shard_map/ppermute | solution.py:24
  41.9 1.2 %collective-permute-start.15 = (bf16[96,16,128]{2,1,0:T(8,128)(2,1)S(1)}, bf16[96,16,128]{2,1,0:T(8,128)(2,1)S(1)}, u32[]{:S(2)}, u32[]{:S(2)}) collective-permute-start(bf16[96,16,128]{2,1,0:T(8,128)(2,1)S(1)} %get-tuple-element.63), channel_id=1, source_target_pairs={{0,6},{1,7},{2,4},{3,5},{4,2},{5,3},{6,0},{7,1},{8,14},{9,15},{10,... | collective-permute-start | bytes 1179656 | tf_op jit(solution)/shard_map/ppermute | solution.py:24
  43.1 1.7 %shard_map.62 = (f32[12,128,128]{2,1,0:T(8,128)S(1)}, f32[12,128,128]{2,1,0:T(8,128)S(1)}, bf16[12,128,128]{2,1,0:T(8,128)(2,1)S(1)}, bf16[12,128,128]{2,1,0:T(8,128)(2,1)S(1)}) custom-call(s32[2]{0:T(128)S(1)} %pad_add_fusion.1.pos, s32[8,64]{1,0:T(8,128)S(1)} %get-tuple-element.71.rows, bf16[112,16,128]{2,1,0:T(8,128)(2,1)S(1)} %get-tuple-element.36.acts.refs_0_, ...), custom_call_target="tpu_custom_call" | custom-call | flops 1 | bytes 1 | tf_op jit(solution)/shard_map/pallas_call | solution.py:32
  44.8 1.6 %collective-permute-start.8 = (bf16[12,128,128]{2,1,0:T(8,128)(2,1)S(1)}, bf16[12,128,128]{2,1,0:T(8,128)(2,1)S(1)}, u32[]{:S(2)}, u32[]{:S(2)}) collective-permute-start(bf16[12,128,128]{2,1,0:T(8,128)(2,1)S(1)} %get-tuple-element.49), channel_id=1, source_target_pairs={{0,8},{8,0},{16,24},{24,16},{1,9},{9,1},{17,25},{25,17},{2,10},{10... | collective-permute-start | bytes 1179656 | tf_op jit(solution)/shard_map/ppermute | solution.py:24
  46.4 2.6 %collective-permute-start.10 = (bf16[12,128,128]{2,1,0:T(8,128)(2,1)S(1)}, bf16[12,128,128]{2,1,0:T(8,128)(2,1)S(1)}, u32[]{:S(2)}, u32[]{:S(2)}) collective-permute-start(bf16[12,128,128]{2,1,0:T(8,128)(2,1)S(1)} %get-tuple-element.54), channel_id=1, source_target_pairs={{0,16},{8,24},{16,0},{24,8},{1,17},{9,25},{17,1},{25,9},{2,18},{10... | collective-permute-start | bytes 1179656 | tf_op jit(solution)/shard_map/ppermute | solution.py:24
  49.0 2.2 %collective-permute-done.13.refs_10_ = bf16[96,16,128]{2,1,0:T(8,128)(2,1)S(1)} collective-permute-done((bf16[96,16,128]{2,1,0:T(8,128)(2,1)S(1)}, bf16[96,16,128]{2,1,0:T(8,128)(2,1)S(1)}, u32[]{:S(2)}, u32[]{:S(2)}) %collective-permute-start.13) | collective-permute-done | bytes 393248 | tf_op jit(solution)/shard_map/ppermute | solution.py:24
  51.3 8.7 %collective-permute-done.14.refs_12_ = bf16[96,16,128]{2,1,0:T(8,128)(2,1)S(1)} collective-permute-done((bf16[96,16,128]{2,1,0:T(8,128)(2,1)S(1)}, bf16[96,16,128]{2,1,0:T(8,128)(2,1)S(1)}, u32[]{:S(2)}, u32[]{:S(2)}) %collective-permute-start.14) | collective-permute-done | bytes 393248 | tf_op jit(solution)/shard_map/ppermute | solution.py:24
  60.5 3.3 %collective-permute-done.8.got = bf16[12,128,128]{2,1,0:T(8,128)(2,1)S(1)} collective-permute-done((bf16[12,128,128]{2,1,0:T(8,128)(2,1)S(1)}, bf16[12,128,128]{2,1,0:T(8,128)(2,1)S(1)}, u32[]{:S(2)}, u32[]{:S(2)}) %collective-permute-start.8) | collective-permute-done | bytes 393248 | tf_op jit(solution)/shard_map/ppermute | solution.py:24
  64.5 4.0 %collective-permute-done.10.got = bf16[12,128,128]{2,1,0:T(8,128)(2,1)S(1)} collective-permute-done((bf16[12,128,128]{2,1,0:T(8,128)(2,1)S(1)}, bf16[12,128,128]{2,1,0:T(8,128)(2,1)S(1)}, u32[]{:S(2)}, u32[]{:S(2)}) %collective-permute-start.10) | collective-permute-done | bytes 393248 | tf_op jit(solution)/shard_map/ppermute | solution.py:24
  69.1 1.5 %shard_map.66 = (f32[4,128,128]{2,1,0:T(8,128)S(1)}, f32[4,128,128]{2,1,0:T(8,128)S(1)}) custom-call(s32[2]{0:T(128)S(1)} %pad_add_fusion.1.pos, s32[8,64]{1,0:T(8,128)S(1)} %get-tuple-element.71.rows, bf16[112,16,128]{2,1,0:T(8,128)(2,1)S(1)} %get-tuple-element.36.acts.refs_0_, bf16[112,16,128]{2,1,0:T(8,128)(2,1)S(1)} %collective-permute-done.refs_1_, ...), custom_call_target="tpu_custom_call" | custom-call | flops 1 | bytes 1 | tf_op jit(solution)/shard_map/pallas_call | solution.py:32
  70.7 4.0 %collective-permute-done.9.refs_1_ = bf16[6,128,128]{2,1,0:T(8,128)(2,1)S(1)} collective-permute-done((bf16[6,128,128]{2,1,0:T(8,128)(2,1)S(1)}, bf16[6,128,128]{2,1,0:T(8,128)(2,1)S(1)}, u32[]{:S(2)}, u32[]{:S(2)}) %collective-permute-start.9) | collective-permute-done | bytes 196640 | tf_op jit(solution)/shard_map/ppermute | solution.py:24
  74.7 2.0 %collective-permute-done.11.refs_3_ = bf16[6,128,128]{2,1,0:T(8,128)(2,1)S(1)} collective-permute-done((bf16[6,128,128]{2,1,0:T(8,128)(2,1)S(1)}, bf16[6,128,128]{2,1,0:T(8,128)(2,1)S(1)}, u32[]{:S(2)}, u32[]{:S(2)}) %collective-permute-start.11) | collective-permute-done | bytes 196640 | tf_op jit(solution)/shard_map/ppermute | solution.py:24
  77.5 12.7 %all_to_all.11 = f32[32,1,128]{2,1,0:T(1,128)S(1)} all-to-all(f32[32,1,128]{2,1,0:T(1,128)S(1)} %bitcast.7), channel_id=1, replica_groups=mesh['tok'=4,'blk'=8] {'tok','blk'}, dimensions={0} | all-to-all | bytes 32768 | tf_op jit(solution)/shard_map/all_to_all | solution.py:383
  (36 shorter events, 5.2 us)
Async XLA Ops:
  0.6 0.7 copy-start.3
  0.6 0.7 copy-start.2
  1.4 1.2 %copy-start = (bf16[16,29568]{1,0:T(8,128)(2,1)S(1)}, bf16[16,29568]{1,0:T(8,128)(2,1)}, u32[]{:S(2)}) copy-start(bf16[16,29568]{1,0:T(8,128)(2,1)} %grad.3) | copy-start | bytes 2838532
  2.6 0.9 %copy-start.1 = (bf16[128,1024]{1,0:T(8,128)(2,1)S(1)}, bf16[128,1024]{1,0:T(8,128)(2,1)}, u32[]{:S(2)}) copy-start(bf16[128,1024]{1,0:T(8,128)(2,1)} %refs_0_.1) | copy-start | bytes 786436
  5.0 19.4 %collective-permute-start.1 = (bf16[160,16,128]{2,1,0:T(8,128)(2,1)S(1)}, bf16[160,16,128]{2,1,0:T(8,128)(2,1)S(1)}, u32[]{:S(2)}, u32[]{:S(2)}) collective-permute-start(bf16[160,16,128]{2,1,0:T(8,128)(2,1)S(1)} %get-tuple-element.38), channel_id=1, source_target_pairs={{0,2},{1,3},{2,0},{3,1},{4,6},{5,7},{6,4},{7,5},{8,10},{9,11},{10,... | collective-permute-start | bytes 1966088 | tf_op jit(solution)/shard_map/ppermute | solution.py:24
  8.0 30.2 %collective-permute-start.2 = (bf16[160,16,128]{2,1,0:T(8,128)(2,1)S(1)}, bf16[160,16,128]{2,1,0:T(8,128)(2,1)S(1)}, u32[]{:S(2)}, u32[]{:S(2)}) collective-permute-start(bf16[160,16,128]{2,1,0:T(8,128)(2,1)S(1)} %get-tuple-element.39), channel_id=1, source_target_pairs={{0,4},{1,5},{2,6},{3,7},{4,0},{5,1},{6,2},{7,3},{8,12},{9,13},{10,... | collective-permute-start | bytes 1966088 | tf_op jit(solution)/shard_map/ppermute | solution.py:24
  9.6 28.7 %collective-permute-start.3 = (bf16[160,16,128]{2,1,0:T(8,128)(2,1)S(1)}, bf16[160,16,128]{2,1,0:T(8,128)(2,1)S(1)}, u32[]{:S(2)}, u32[]{:S(2)}) collective-permute-start(bf16[160,16,128]{2,1,0:T(8,128)(2,1)S(1)} %get-tuple-element.40), channel_id=1, source_target_pairs={{0,6},{1,7},{2,4},{3,5},{4,2},{5,3},{6,0},{7,1},{8,14},{9,15},{10,... | collective-permute-start | bytes 1966088 | tf_op jit(solution)/shard_map/ppermute | solution.py:24
  10.5 13.2 %collective-permute-start.4 = (bf16[128,16,128]{2,1,0:T(8,128)(2,1)S(1)}, bf16[128,16,128]{2,1,0:T(8,128)(2,1)S(1)}, u32[]{:S(2)}, u32[]{:S(2)}) collective-permute-start(bf16[128,16,128]{2,1,0:T(8,128)(2,1)S(1)} %get-tuple-element.43), channel_id=1, source_target_pairs={{0,8},{8,0},{16,24},{24,16},{1,9},{9,1},{17,25},{25,17},{2,10},{10... | collective-permute-start | bytes 1572872 | tf_op jit(solution)/shard_map/ppermute | solution.py:24
  12.6 11.8 %collective-permute-start = (bf16[112,16,128]{2,1,0:T(8,128)(2,1)S(1)}, bf16[112,16,128]{2,1,0:T(8,128)(2,1)S(1)}, u32[]{:S(2)}, u32[]{:S(2)}) collective-permute-start(bf16[112,16,128]{2,1,0:T(8,128)(2,1)S(1)} %get-tuple-element.37), channel_id=1, source_target_pairs={{0,1},{1,0},{2,3},{3,2},{4,5},{5,4},{6,7},{7,6},{8,9},{9,8},{10,11... | collective-permute-start | bytes 1376264 | tf_op jit(solution)/shard_map/ppermute | solution.py:24
  38.3 2.3 %collective-permute-start.5 = (bf16[160,16,128]{2,1,0:T(8,128)(2,1)S(1)}, bf16[160,16,128]{2,1,0:T(8,128)(2,1)S(1)}, u32[]{:S(2)}, u32[]{:S(2)}) collective-permute-start(bf16[160,16,128]{2,1,0:T(8,128)(2,1)S(1)} %collective-permute-done.1.refs_2_), channel_id=1, source_target_pairs={{0,1},{1,0},{2,3},{3,2},{4,5},{5,4},{6,7},{7,6},{8,9},{9,8},{10,11... | collective-permute-start | bytes 1966088 | tf_op jit(solution)/shard_map/ppermute | solution.py:24
  38.3 3.6 %collective-permute-start.6 = (bf16[160,16,128]{2,1,0:T(8,128)(2,1)S(1)}, bf16[160,16,128]{2,1,0:T(8,128)(2,1)S(1)}, u32[]{:S(2)}, u32[]{:S(2)}) collective-permute-start(bf16[160,16,128]{2,1,0:T(8,128)(2,1)S(1)} %collective-permute-done.2.refs_4_), channel_id=1, source_target_pairs={{0,1},{1,0},{2,3},{3,2},{4,5},{5,4},{6,7},{7,6},{8,9},{9,8},{10,11... | collective-permute-start | bytes 1966088 | tf_op jit(solution)/shard_map/ppermute | solution.py:24
  38.8 4.3 %collective-permute-start.7 = (bf16[160,16,128]{2,1,0:T(8,128)(2,1)S(1)}, bf16[160,16,128]{2,1,0:T(8,128)(2,1)S(1)}, u32[]{:S(2)}, u32[]{:S(2)}) collective-permute-start(bf16[160,16,128]{2,1,0:T(8,128)(2,1)S(1)} %collective-permute-done.3.refs_6_), channel_id=1, source_target_pairs={{0,1},{1,0},{2,3},{3,2},{4,5},{5,4},{6,7},{7,6},{8,9},{9,8},{10,11... | collective-permute-start | bytes 1966088 | tf_op jit(solution)/shard_map/ppermute | solution.py:24
  38.8 7.7 %collective-permute-start.12 = (bf16[80,16,128]{2,1,0:T(8,128)(2,1)S(1)}, bf16[80,16,128]{2,1,0:T(8,128)(2,1)S(1)}, u32[]{:S(2)}, u32[]{:S(2)}) collective-permute-start(bf16[80,16,128]{2,1,0:T(8,128)(2,1)S(1)} %get-tuple-element.60), channel_id=1, source_target_pairs={{0,1},{1,0},{2,3},{3,2},{4,5},{5,4},{6,7},{7,6},{8,9},{9,8},{10,11... | collective-permute-start | bytes 983048 | tf_op jit(solution)/shard_map/ppermute | solution.py:24
  39.3 12.0 %collective-permute-start.13 = (bf16[96,16,128]{2,1,0:T(8,128)(2,1)S(1)}, bf16[96,16,128]{2,1,0:T(8,128)(2,1)S(1)}, u32[]{:S(2)}, u32[]{:S(2)}) collective-permute-start(bf16[96,16,128]{2,1,0:T(8,128)(2,1)S(1)} %get-tuple-element.61), channel_id=1, source_target_pairs={{0,2},{1,3},{2,0},{3,1},{4,6},{5,7},{6,4},{7,5},{8,10},{9,11},{10,... | collective-permute-start | bytes 1179656 | tf_op jit(solution)/shard_map/ppermute | solution.py:24
  40.5 19.4 %collective-permute-start.14 = (bf16[96,16,128]{2,1,0:T(8,128)(2,1)S(1)}, bf16[96,16,128]{2,1,0:T(8,128)(2,1)S(1)}, u32[]{:S(2)}, u32[]{:S(2)}) collective-permute-start(bf16[96,16,128]{2,1,0:T(8,128)(2,1)S(1)} %get-tuple-element.62), channel_id=1, source_target_pairs={{0,4},{1,5},{2,6},{3,7},{4,0},{5,1},{6,2},{7,3},{8,12},{9,13},{10,... | collective-permute-start | bytes 1179656 | tf_op jit(solution)/shard_map/ppermute | solution.py:24
  41.9 18.1 %collective-permute-start.15 = (bf16[96,16,128]{2,1,0:T(8,128)(2,1)S(1)}, bf16[96,16,128]{2,1,0:T(8,128)(2,1)S(1)}, u32[]{:S(2)}, u32[]{:S(2)}) collective-permute-start(bf16[96,16,128]{2,1,0:T(8,128)(2,1)S(1)} %get-tuple-element.63), channel_id=1, source_target_pairs={{0,6},{1,7},{2,4},{3,5},{4,2},{5,3},{6,0},{7,1},{8,14},{9,15},{10,... | collective-permute-start | bytes 1179656 | tf_op jit(solution)/shard_map/ppermute | solution.py:24
  44.8 19.0 %collective-permute-start.8 = (bf16[12,128,128]{2,1,0:T(8,128)(2,1)S(1)}, bf16[12,128,128]{2,1,0:T(8,128)(2,1)S(1)}, u32[]{:S(2)}, u32[]{:S(2)}) collective-permute-start(bf16[12,128,128]{2,1,0:T(8,128)(2,1)S(1)} %get-tuple-element.49), channel_id=1, source_target_pairs={{0,8},{8,0},{16,24},{24,16},{1,9},{9,1},{17,25},{25,17},{2,10},{10... | collective-permute-start | bytes 1179656 | tf_op jit(solution)/shard_map/ppermute | solution.py:24
  46.4 22.1 %collective-permute-start.10 = (bf16[12,128,128]{2,1,0:T(8,128)(2,1)S(1)}, bf16[12,128,128]{2,1,0:T(8,128)(2,1)S(1)}, u32[]{:S(2)}, u32[]{:S(2)}) collective-permute-start(bf16[12,128,128]{2,1,0:T(8,128)(2,1)S(1)} %get-tuple-element.54), channel_id=1, source_target_pairs={{0,16},{8,24},{16,0},{24,8},{1,17},{9,25},{17,1},{25,9},{2,18},{10... | collective-permute-start | bytes 1179656 | tf_op jit(solution)/shard_map/ppermute | solution.py:24
  60.0 9.1 %collective-permute-start.16 = (bf16[96,16,128]{2,1,0:T(8,128)(2,1)S(1)}, bf16[96,16,128]{2,1,0:T(8,128)(2,1)S(1)}, u32[]{:S(2)}, u32[]{:S(2)}) collective-permute-start(bf16[96,16,128]{2,1,0:T(8,128)(2,1)S(1)} %collective-permute-done.13.refs_10_), channel_id=1, source_target_pairs={{0,1},{1,0},{2,3},{3,2},{4,5},{5,4},{6,7},{7,6},{8,9},{9,8},{10,11... | collective-permute-start | bytes 1179656 | tf_op jit(solution)/shard_map/ppermute | solution.py:24
  60.0 9.1 %collective-permute-start.17 = (bf16[96,16,128]{2,1,0:T(8,128)(2,1)S(1)}, bf16[96,16,128]{2,1,0:T(8,128)(2,1)S(1)}, u32[]{:S(2)}, u32[]{:S(2)}) collective-permute-start(bf16[96,16,128]{2,1,0:T(8,128)(2,1)S(1)} %collective-permute-done.14.refs_12_), channel_id=1, source_target_pairs={{0,1},{1,0},{2,3},{3,2},{4,5},{5,4},{6,7},{7,6},{8,9},{9,8},{10,11... | collective-permute-start | bytes 1179656 | tf_op jit(solution)/shard_map/ppermute | solution.py:24
  60.5 8.6 %collective-permute-start.18 = (bf16[96,16,128]{2,1,0:T(8,128)(2,1)S(1)}, bf16[96,16,128]{2,1,0:T(8,128)(2,1)S(1)}, u32[]{:S(2)}, u32[]{:S(2)}) collective-permute-start(bf16[96,16,128]{2,1,0:T(8,128)(2,1)S(1)} %collective-permute-done.15.refs_14_), channel_id=1, source_target_pairs={{0,1},{1,0},{2,3},{3,2},{4,5},{5,4},{6,7},{7,6},{8,9},{9,8},{10,11... | collective-permute-start | bytes 1179656 | tf_op jit(solution)/shard_map/ppermute | solution.py:24
  63.9 10.8 %collective-permute-start.9 = (bf16[6,128,128]{2,1,0:T(8,128)(2,1)S(1)}, bf16[6,128,128]{2,1,0:T(8,128)(2,1)S(1)}, u32[]{:S(2)}, u32[]{:S(2)}) collective-permute-start(bf16[6,128,128]{2,1,0:T(8,128)(2,1)S(1)} %get-tuple-element.51), channel_id=1, source_target_pairs={{0,16},{8,24},{16,0},{24,8},{1,17},{9,25},{17,1},{25,9},{2,18},{10... | collective-permute-start | bytes 589832 | tf_op jit(solution)/shard_map/ppermute | solution.py:24
  68.6 8.1 %collective-permute-start.11 = (bf16[6,128,128]{2,1,0:T(8,128)(2,1)S(1)}, bf16[6,128,128]{2,1,0:T(8,128)(2,1)S(1)}, u32[]{:S(2)}, u32[]{:S(2)}) collective-permute-start(bf16[6,128,128]{2,1,0:T(8,128)(2,1)S(1)} %get-tuple-element.56), channel_id=1, source_target_pairs={{0,8},{8,0},{16,24},{24,16},{1,9},{9,1},{17,25},{25,17},{2,10},{10... | collective-permute-start | bytes 589832 | tf_op jit(solution)/shard_map/ppermute | solution.py:24
  76.7 13.5 %collective-permute-start.19 = (f32[4,128,128]{2,1,0:T(8,128)S(1)}, f32[4,128,128]{2,1,0:T(8,128)S(1)}, u32[]{:S(2)}, u32[]{:S(2)}) collective-permute-start(f32[4,128,128]{2,1,0:T(8,128)S(1)} %get-tuple-element.69), channel_id=1, source_target_pairs={{0,16},{8,24},{16,0},{24,8},{1,17},{9,25},{17,1},{25,9},{2,18},{10... | collective-permute-start | bytes 786440 | tf_op jit(solution)/shard_map/ppermute | solution.py:24
